TPU v7x, 32 devices: a whole 2x2x4 slice. The times are simulated.
32 devices in a mesh: fsdp: 4 (over y, x), ctx: 8 (over z, core).
Axes of the slice: x: 2, y: 2, z: 4, core: 2. Of those that a mesh axis runs over, the one named last changes fastest.
Arguments:
- inputs: bfloat16 [4, 2048, 768], P('fsdp', 'ctx'), may hold values from -6 to 6
- positions: int32 [4, 2048], P('fsdp', 'ctx'), may hold values from 0 to 2047, as said below
- in_weight: bfloat16 [768, 2304], P('fsdp'), may hold values from -0.21875 to 0.21875
- in_bias: bfloat16 [2304], P('fsdp'), may hold values from -0.3125 to 0.3125
- out_weight: bfloat16 [768, 768], P('fsdp'), may hold values from -0.109375 to 0.109375
- out_bias: bfloat16 [768], P('fsdp'), may hold values from -4 to 4
- up_weight: bfloat16 [768, 3072], P('fsdp'), may hold values from -0.21875 to 0.21875
- up_bias: bfloat16 [3072], P('fsdp'), may hold values from -6 to 6
- down_weight: bfloat16 [3072, 768], P('fsdp'), may hold values from -0.109375 to 0.109375
- down_bias: bfloat16 [768], P('fsdp'), may hold values from -4 to 4
- first_gain: bfloat16 [768], P('fsdp'), may hold values from 0.25 to 1.75
- first_shift: bfloat16 [768], P('fsdp'), may hold values from -4 to 4
- second_gain: bfloat16 [768], P('fsdp'), may hold values from 0.25 to 1.75
- second_shift: bfloat16 [768], P('fsdp'), may hold values from -4 to 4
- out_grad: bfloat16 [4, 2048, 768], P('fsdp', 'ctx'), may hold values from -6 to 6
Outputs:
- output: bfloat16 [4, 2048, 768], P('fsdp', 'ctx')
- input_gradient: float32 [4, 2048, 768], P('fsdp', 'ctx')
- in_weight_gradient: float32 [768, 2304], P('fsdp')
- in_bias_gradient: float32 [2304], P('fsdp')
- out_weight_gradient: float32 [768, 768], P('fsdp')
- out_bias_gradient: float32 [768], P('fsdp')
- up_weight_gradient: float32 [768, 3072], P('fsdp')
- up_bias_gradient: float32 [3072], P('fsdp')
- down_weight_gradient: float32 [3072, 768], P('fsdp')
- down_bias_gradient: float32 [768], P('fsdp')
- first_gain_gradient: float32 [768], P('fsdp')
- first_shift_gradient: float32 [768], P('fsdp')
- second_gain_gradient: float32 [768], P('fsdp')
- second_shift_gradient: float32 [768], P('fsdp')
Inputs may be any that keep to these rules, and one draw needn't show every extreme that they name: Each row holds every position of its sequence once, in runs of 128 consecutive rising positions that start at multiples of 128; the order of the runs differs from row to row.
All inputs are finite; a program needn't handle non-finite values.
Results may differ from a plain program's by a relative error of at most 0.018.
Values may be sent and summed in bfloat16 or wider, within the bound.
No kernel may reach another device: no remote copies, remote signals or barrier semaphores. Data moves between devices by JAX's collectives and lax.ppermute only.
A program may use at most 192 MiB of HBM per device.

v0:
```python
import math
import jax
import jax.numpy as jnp
from jax import lax
from jax.sharding import PartitionSpec as P

HEAD = 64
ROT = 16
NEG = -1e30
EPS = 1e-05


def from_behind(x, axis, by):
    size = lax.axis_size(axis)
    return lax.ppermute(x, axis, [(i, (i + by) % size) for i in range(size)])


def layer_norm(values, gain, shift):
    mean = jnp.mean(values, -1, keepdims=True)
    centred = values - mean
    spread = jnp.mean(centred * centred, -1, keepdims=True)
    return centred * lax.rsqrt(spread + EPS) * gain + shift


def turn_tables(positions):
    ladder = 10000.0 ** (-jnp.arange(0, ROT, 2, dtype=jnp.float32) / ROT)
    angle = positions.astype(jnp.float32)[..., None] * ladder
    angle = jnp.concatenate([angle, angle], -1)
    return (jnp.cos(angle), jnp.sin(angle))


def rotate(values, cosine, sine):
    half = ROT // 2
    part = values[..., :ROT]
    turned = jnp.concatenate([-part[..., half:], part[..., :half]], -1)
    part = part * cosine[..., None, :] + turned * sine[..., None, :]
    return jnp.concatenate([part, values[..., ROT:]], -1)


def across(left, right):
    return lax.dot_general(
        left, right, (((0,), (0,)), ((), ())), preferred_element_type=jnp.float32
    )


def against(left, right):
    return lax.dot_general(
        left, right, (((1,), (1,)), ((), ())), preferred_element_type=jnp.float32
    )


def softmax_step(carry, queries, query_pos, keys, values, key_pos, scale):
    peak, total, summed = carry
    scores = jnp.einsum("qhd,khd->hqk", queries, keys, preferred_element_type=jnp.float32) * scale
    allowed = (key_pos[None, :] <= query_pos[:, None])[None]
    new_peak = jnp.maximum(peak, jnp.max(jnp.where(allowed, scores, NEG), -1))
    weights = jnp.where(allowed, jnp.exp(scores - new_peak[..., None]), 0.0)
    fade = jnp.exp(peak - new_peak)
    total = total * fade + jnp.sum(weights, -1)
    added = jnp.einsum(
        "hqk,khd->qhd", weights.astype(jnp.bfloat16), values, preferred_element_type=jnp.float32
    )
    summed = summed * jnp.transpose(fade)[:, :, None] + added
    return (new_peak, total, summed)


def gradient_step(
    state, queries, query_pos, outs_back, log_total, spread, keys, values, key_pos, scale
):
    back_query, back_key, back_value = state
    scores = jnp.einsum("qhd,khd->hqk", queries, keys, preferred_element_type=jnp.float32) * scale
    allowed = (key_pos[None, :] <= query_pos[:, None])[None]
    probs = jnp.where(allowed, jnp.exp(scores - log_total[..., None]), 0.0)
    back_probs = jnp.einsum("qhd,khd->hqk", outs_back, values, preferred_element_type=jnp.float32)
    back_scores = (probs * (back_probs - spread[..., None])).astype(jnp.bfloat16)
    back_query = (
        back_query
        + jnp.einsum("hqk,khd->qhd", back_scores, keys, preferred_element_type=jnp.float32) * scale
    )
    back_key = (
        back_key
        + jnp.einsum("hqk,qhd->khd", back_scores, queries, preferred_element_type=jnp.float32)
        * scale
    )
    back_value = back_value + jnp.einsum(
        "hqk,qhd->khd", probs.astype(jnp.bfloat16), outs_back, preferred_element_type=jnp.float32
    )
    return (back_query, back_key, back_value)


def on_device(
    inputs,
    positions,
    in_weight,
    in_bias,
    out_weight,
    out_bias,
    up_weight,
    up_bias,
    down_weight,
    down_bias,
    first_gain,
    first_shift,
    second_gain,
    second_shift,
    out_grad,
):
    gathered = (
        lax.all_gather(in_weight, "fsdp", axis=0, tiled=True),
        lax.all_gather(in_bias, "fsdp", axis=0, tiled=True),
        lax.all_gather(out_weight, "fsdp", axis=0, tiled=True),
        lax.all_gather(out_bias, "fsdp", axis=0, tiled=True),
        lax.all_gather(up_weight, "fsdp", axis=0, tiled=True),
        lax.all_gather(up_bias, "fsdp", axis=0, tiled=True),
        lax.all_gather(down_weight, "fsdp", axis=0, tiled=True),
        lax.all_gather(down_bias, "fsdp", axis=0, tiled=True),
        lax.all_gather(first_gain, "fsdp", axis=0, tiled=True),
        lax.all_gather(first_shift, "fsdp", axis=0, tiled=True),
        lax.all_gather(second_gain, "fsdp", axis=0, tiled=True),
        lax.all_gather(second_shift, "fsdp", axis=0, tiled=True),
    )
    (
        full_in,
        full_in_bias,
        full_out,
        full_out_bias,
        full_up,
        full_up_bias,
        full_down,
        full_down_bias,
        gain_one,
        shift_one,
        gain_two,
        shift_two,
    ) = gathered
    tokens = inputs.shape[1]
    width = inputs.shape[2]
    heads = width // HEAD
    scale = 1.0 / math.sqrt(HEAD)
    query_pos = positions[0]
    all_pos = lax.all_gather(query_pos, "ctx", axis=0, tiled=True)
    resid = inputs[0].astype(jnp.float32)

    def norms(values, gain_a, shift_a, gain_b, shift_b):
        return (layer_norm(values, gain_a, shift_a), layer_norm(values, gain_b, shift_b))

    (normed_one, normed_two), norm_back = jax.vjp(
        norms,
        resid,
        gain_one.astype(jnp.float32),
        shift_one.astype(jnp.float32),
        gain_two.astype(jnp.float32),
        shift_two.astype(jnp.float32),
    )
    first = normed_one.astype(jnp.bfloat16)
    second = normed_two.astype(jnp.bfloat16)
    projected = jnp.dot(first, full_in, preferred_element_type=jnp.float32) + full_in_bias.astype(
        jnp.float32
    )
    projected = projected.reshape(tokens, 3, heads, HEAD)
    cosine, sine = turn_tables(query_pos)
    queries = rotate(projected[:, 0], cosine, sine).astype(jnp.bfloat16)
    keys = rotate(projected[:, 1], cosine, sine).astype(jnp.bfloat16)
    values = projected[:, 2].astype(jnp.bfloat16)
    start_state = (
        jnp.full((heads, tokens), NEG, jnp.float32),
        jnp.zeros((heads, tokens), jnp.float32),
        jnp.zeros((tokens, heads, HEAD), jnp.float32),
    )
    carry = start_state
    key_piece = lax.all_gather(keys, "ctx", axis=0, tiled=True)
    value_piece = lax.all_gather(values, "ctx", axis=0, tiled=True)
    count = key_piece.shape[0]
    size = 512

    def one_block(inner, offset):
        key_block = lax.dynamic_slice_in_dim(key_piece, offset, size, 0)
        value_block = lax.dynamic_slice_in_dim(value_piece, offset, size, 0)
        key_pos = lax.dynamic_slice_in_dim(all_pos, offset, size, 0)
        result = softmax_step(inner, queries, query_pos, key_block, value_block, key_pos, scale)
        return (result, None)

    carry, _ = lax.scan(one_block, carry, jnp.arange(0, count, size, dtype=jnp.int32))
    peak, total, summed = carry
    attended = summed / jnp.transpose(total)[:, :, None]
    log_total = peak + jnp.log(total)
    mixed = attended.reshape(tokens, width).astype(jnp.bfloat16)
    up = jnp.dot(second, full_up, preferred_element_type=jnp.float32) + full_up_bias.astype(
        jnp.float32
    )
    activated, gelu_back = jax.vjp(lambda value: jax.nn.gelu(value, approximate=False), up)
    activated = activated.astype(jnp.bfloat16)
    branch_attn = jnp.dot(
        mixed, full_out, preferred_element_type=jnp.float32
    ) + full_out_bias.astype(jnp.float32)
    branch_ff = jnp.dot(
        activated, full_down, preferred_element_type=jnp.float32
    ) + full_down_bias.astype(jnp.float32)
    output = resid + branch_attn + branch_ff
    cotangent = out_grad[0]
    back_out = cotangent.astype(jnp.float32)
    bias_sum = jnp.sum(back_out, 0)
    out_weight_part = across(mixed, cotangent)
    down_weight_part = across(activated, cotangent)
    back_mixed = against(cotangent, full_out).astype(jnp.bfloat16)
    back_active = against(cotangent, full_down)
    back_up = gelu_back(back_active)[0].astype(jnp.bfloat16)
    up_weight_part = across(second, back_up)
    up_bias_part = jnp.sum(back_up.astype(jnp.float32), 0)
    back_second = against(back_up, full_up)
    outs_back = back_mixed.reshape(tokens, heads, HEAD)
    spread = jnp.einsum("qhd,qhd->hq", outs_back.astype(jnp.float32), attended)
    cycle_size = lax.axis_size("ctx")
    here = lax.axis_index("ctx")
    zeros = jnp.zeros((tokens, heads, HEAD), jnp.float32)

    def key_turn(turn, state):
        moving_key, moving_value, back_key, back_value, back_query = state
        owner = (here - turn) % cycle_size
        key_pos = lax.dynamic_slice_in_dim(all_pos, owner * tokens, tokens, 0)
        back_query, back_key, back_value = gradient_step(
            (back_query, back_key, back_value),
            queries,
            query_pos,
            outs_back,
            log_total,
            spread,
            moving_key,
            moving_value,
            key_pos,
            scale,
        )
        moving_key, moving_value = from_behind((moving_key, moving_value), "ctx", 1)
        back_key, back_value = (
            from_behind(back_key.astype(jnp.bfloat16), "ctx", 1).astype(back_key.dtype),
            from_behind(back_value.astype(jnp.bfloat16), "ctx", 1).astype(back_value.dtype),
        )
        return (moving_key, moving_value, back_key, back_value, back_query)

    final = lax.fori_loop(0, cycle_size, key_turn, (keys, values, zeros, zeros, zeros))
    back_query, back_key, back_value = (final[4], final[2], final[3])
    back_query = rotate(back_query, cosine, -sine)
    back_key = rotate(back_key, cosine, -sine)
    back_projected = (
        jnp.stack([back_query, back_key, back_value], 1)
        .reshape(tokens, 3 * width)
        .astype(jnp.bfloat16)
    )
    in_weight_part = across(first, back_projected)
    in_bias_part = jnp.sum(back_projected.astype(jnp.float32), 0)
    back_first = against(back_projected, full_in)
    back_resid, gain_one_part, shift_one_part, gain_two_part, shift_two_part = norm_back(
        (back_first, back_second)
    )
    input_gradient = back_out + back_resid
    shares = (
        lax.psum_scatter(
            in_weight_part.astype(jnp.bfloat16), "fsdp", scatter_dimension=0, tiled=True
        ).astype(jnp.float32),
        lax.psum_scatter(
            in_bias_part.astype(jnp.bfloat16), "fsdp", scatter_dimension=0, tiled=True
        ).astype(jnp.float32),
        lax.psum_scatter(
            out_weight_part.astype(jnp.bfloat16), "fsdp", scatter_dimension=0, tiled=True
        ).astype(jnp.float32),
        lax.psum_scatter(
            bias_sum.astype(jnp.bfloat16), "fsdp", scatter_dimension=0, tiled=True
        ).astype(jnp.float32),
        lax.psum_scatter(
            up_weight_part.astype(jnp.bfloat16), "fsdp", scatter_dimension=0, tiled=True
        ).astype(jnp.float32),
        lax.psum_scatter(
            up_bias_part.astype(jnp.bfloat16), "fsdp", scatter_dimension=0, tiled=True
        ).astype(jnp.float32),
        lax.psum_scatter(
            down_weight_part.astype(jnp.bfloat16), "fsdp", scatter_dimension=0, tiled=True
        ).astype(jnp.float32),
        lax.psum_scatter(
            gain_one_part.astype(jnp.bfloat16), "fsdp", scatter_dimension=0, tiled=True
        ).astype(jnp.float32),
        lax.psum_scatter(
            shift_one_part.astype(jnp.bfloat16), "fsdp", scatter_dimension=0, tiled=True
        ).astype(jnp.float32),
        lax.psum_scatter(
            gain_two_part.astype(jnp.bfloat16), "fsdp", scatter_dimension=0, tiled=True
        ).astype(jnp.float32),
        lax.psum_scatter(
            shift_two_part.astype(jnp.bfloat16), "fsdp", scatter_dimension=0, tiled=True
        ).astype(jnp.float32),
    )
    totals = (
        lax.psum(shares[0].astype(jnp.bfloat16), "ctx").astype(jnp.float32),
        lax.psum(shares[1].astype(jnp.bfloat16), "ctx").astype(jnp.float32),
        lax.psum(shares[2].astype(jnp.bfloat16), "ctx").astype(jnp.float32),
        lax.psum(shares[3].astype(jnp.bfloat16), "ctx").astype(jnp.float32),
        lax.psum(shares[4].astype(jnp.bfloat16), "ctx").astype(jnp.float32),
        lax.psum(shares[5].astype(jnp.bfloat16), "ctx").astype(jnp.float32),
        lax.psum(shares[6].astype(jnp.bfloat16), "ctx").astype(jnp.float32),
        lax.psum(shares[7].astype(jnp.bfloat16), "ctx").astype(jnp.float32),
        lax.psum(shares[8].astype(jnp.bfloat16), "ctx").astype(jnp.float32),
        lax.psum(shares[9].astype(jnp.bfloat16), "ctx").astype(jnp.float32),
        lax.psum(shares[10].astype(jnp.bfloat16), "ctx").astype(jnp.float32),
    )
    return (
        output.astype(jnp.bfloat16)[None],
        input_gradient[None],
        totals[0],
        totals[1],
        totals[2],
        totals[3],
        totals[4],
        totals[5],
        totals[6],
        totals[3],
        totals[7],
        totals[8],
        totals[9],
        totals[10],
    )


def solution(mesh):
    return jax.shard_map(
        on_device,
        mesh=mesh,
        in_specs=(
            P("fsdp", "ctx", None),
            P("fsdp", "ctx"),
            P("fsdp", None),
            P("fsdp"),
            P("fsdp", None),
            P("fsdp"),
            P("fsdp", None),
            P("fsdp"),
            P("fsdp", None),
            P("fsdp"),
            P("fsdp"),
            P("fsdp"),
            P("fsdp"),
            P("fsdp"),
            P("fsdp", "ctx", None),
        ),
        out_specs=(
            P("fsdp", "ctx", None),
            P("fsdp", "ctx", None),
            P("fsdp", None),
            P("fsdp"),
            P("fsdp", None),
            P("fsdp"),
            P("fsdp", None),
            P("fsdp"),
            P("fsdp", None),
            P("fsdp"),
            P("fsdp"),
            P("fsdp"),
            P("fsdp"),
            P("fsdp"),
        ),
        check_vma=False,
    )
```

profile of v0, /device:TPU:0, one launch (start us, length us, event | category | flops | bytes accessed | tf_op | source)
XLA Modules:
  0.0 707.0 jit_solution(10681487738134994407)
XLA Ops:
  14.8 18.4 %all-reduce.17 = (bf16[768]{0:T(1024)(128)(2,1)}, bf16[768]{0:T(1024)(128)(2,1)}, bf16[2304]{0:T(1024)(128)(2,1)S(1)}, bf16[768]{0:T(1024)(128)(2,1)S(1)}, bf16[768]{0:T(1024)(128)(2,1)S(1)}) all-reduce(bf16[768]{0:T(1024)(128)(2,1)S(1)} %dynamic-update-slice.5, ...), channel_id=1, replica_groups=mesh['fsdp'=4,'ctx'=8] {'fsdp'}, use_global_device_ids=true, to_apply=%add.5 | all-reduce | flops 5376 | bytes 21504
  37.1 22.8 %all-gather.10.cloned.1.call-done = bf16[768,2304]{1,0:T(8,128)(2,1)} async-done(((bf16[192,2304]{1,0:T(8,128)(2,1)}), bf16[768,2304]{1,0:T(8,128)(2,1)}) %all-gather.10.cloned.1.call-update) | async-done | bytes 3538960 | tf_op jit(solution)/shard_map/all_gather | solution.py:109
  59.9 4.7 convolution_add_fusion
  71.0 12.8 %all-gather = s32[1,2048]{1,0:T(1,128)} all-gather(s32[1,256]{1,0:T(1,128)} %param.20), channel_id=2, replica_groups=mesh['fsdp'=4,'ctx'=8] {'ctx'}, dimensions={1}, use_global_device_ids=true | all-gather | bytes 9216 | tf_op jit(solution)/shard_map/all_gather | solution.py:141
  85.9 8.1 %all-gather.2 = bf16[4,1,768]{2,1,0:T(2,128)(2,1)S(1)} all-gather(bf16[1,1,768]{2,1,0:T(2,128)(2,1)S(1)} %reshape.293), channel_id=1, replica_groups=mesh['fsdp'=4,'ctx'=8] {'fsdp'}, dimensions={0}, use_global_device_ids=true | all-gather | bytes 7680 | tf_op jit(solution)/shard_map/all_gather | solution.py:114
  94.1 13.7 %all-gather.12.cloned.1.call-done = bf16[2048,12,64]{0,2,1:T(8,128)(2,1)} async-done(((bf16[256,12,64]{0,2,1:T(8,128)(2,1)}), bf16[2048,12,64]{0,2,1:T(8,128)(2,1)}) %all-gather.12.cloned.1.call-update) | async-done | bytes 3145744 | tf_op jit(solution)/shard_map/all_gather | solution.py:171
  107.7 41.4 %all-gather.20.cloned.1.call-done = bf16[2048,1,12,64]{0,3,2,1:T(8,128)(2,1)} async-done(((bf16[256,1,12,64]{0,3,2,1:T(8,128)(2,1)}), bf16[2048,1,12,64]{0,3,2,1:T(8,128)(2,1)}) %all-gather.20.cloned.1.call-update) | async-done | bytes 3145744 | tf_op jit(solution)/shard_map/all_gather | solution.py:172
  149.1 64.1 %while.39 = (s32[]{:T(128)}, f32[12,256]{1,0:T(8,128)S(1)}, f32[12,256]{1,0:T(8,128)S(1)}, f32[256,12,64]{0,2,1:T(8,128)S(1)}, s32[4]{0:T(128)S(1)}, /*index=5*/...) while((s32[]{:T(128)}, f32[12,256]{1,0:T(8,128)S(1)}, ...), condition=%wide.region_5.6_spmd.clone, body=%wide.region_2.5_spmd.clone.sunk | while | flops 420694016 | bytes 48307420 | solution.py:183
  153.2 5.7 fusion.173
  158.9 4.8 fusion.177
  169.2 5.5 fusion.173
  174.7 4.8 fusion.177
  185.8 5.5 fusion.173
  191.3 4.8 fusion.177
  201.6 5.4 fusion.173
  207.1 4.7 fusion.177
  215.2 11.6 %multiply_convert_fusion.1 = (bf16[256,3072]{1,0:T(8,128)(2,1)S(1)}, f32[256,3072]{1,0:T(8,128)}, f32[256,3072]{1,0:T(8,128)}) fusion(f32[3072]{0:T(1024)S(1)} %bitcast.232, bf16[768,3072]{1,0:T(8,128)(2,1)} %all-gather.16.cloned.1.call-done, bf16[1,256,768]{2,1,0:T(8,128)(2,1)S(1)} %copy-done.3, f32[768]{0:T(1024)S(1)} %convert_element_type.251, ...), kind=kOutput, calls=%fused_computation.54 | convolution fusion | flops 1261043712 | bytes 12996608 | tf_op jit(solution)/shard_map/dot_general | solution.py:188
  226.7 38.2 %all-gather.18.cloned.1.call-done = bf16[3072,768]{1,0:T(8,128)(2,1)} async-done(((bf16[768,768]{1,0:T(8,128)(2,1)}), bf16[3072,768]{1,0:T(8,128)(2,1)}) %all-gather.18.cloned.1.call-update) | async-done | bytes 4718608 | tf_op jit(solution)/shard_map/all_gather | solution.py:115
  264.9 6.8 fusion.119
  272.9 3.7 convolution_convert_fusion.1
  276.7 17.6 %all-gather.14.cloned.1.call-done = bf16[768,768]{1,0:T(8,128)(2,1)} async-done(((bf16[192,768]{1,0:T(8,128)(2,1)}), bf16[768,768]{1,0:T(8,128)(2,1)}) %all-gather.14.cloned.1.call-update) | async-done | bytes 1179664 | tf_op jit(solution)/shard_map/all_gather | solution.py:111
  294.4 2.5 convolution_convert_fusion.4
  300.7 3.5 convolution_convert_fusion
  307.7 244.7 %while.40 = (s32[]{:T(128)}, bf16[256,12,64]{0,2,1:T(8,128)(2,1)}, bf16[256,12,64]{0,2,1:T(8,128)(2,1)}, f32[256,12,64]{0,2,1:T(8,128)S(1)}, f32[256,12,64]{0,2,...) while((s32[]{:T(128)}, bf16[256,12,64]{0,2,1:T(8,128)(2,1)}, ...), condition=%wide.region_9.10_spmd.clone, body=%wide.region_8.9_spmd.clone.sunk | while | flops 513605632 | bytes 40837772 | solution.py:240
  316.4 2.6 fusion.190
  326.8 3.1 collective-permute-done.3
  334.1 4.2 collective-permute-done.1
  346.9 2.6 fusion.190
  352.6 3.6 collective-permute-done.2
  357.3 3.1 collective-permute-done.3
  364.7 4.2 collective-permute-done.1
  377.6 2.6 fusion.190
  381.9 5.1 collective-permute-done.2
  388.0 3.1 collective-permute-done.3
  395.4 4.2 collective-permute-done.1
  404.6 2.5 multiply_convert_fusion.3
  408.2 2.7 fusion.190
  412.6 5.0 collective-permute-done.2
  418.6 3.1 collective-permute-done.3
  426.0 4.2 collective-permute-done.1
  438.8 2.6 fusion.190
  443.1 5.1 collective-permute-done.2
  449.2 3.1 collective-permute-done.3
  456.6 4.2 collective-permute-done.1
  469.4 2.6 fusion.190
  473.6 5.1 collective-permute-done.2
  479.8 3.1 collective-permute-done.3
  487.1 4.2 collective-permute-done.1
  499.9 2.6 fusion.190
  504.2 5.1 collective-permute-done.2
  510.3 3.1 collective-permute-done.3
  517.7 4.2 collective-permute-done.1
  530.5 2.6 fusion.190
  534.7 5.1 collective-permute-done.2
  540.9 3.1 collective-permute-done.3
  548.2 4.2 collective-permute-done.1
  556.2 3.2 convolution_convert_fusion.2
  563.0 4.8 fusion.121
  570.0 34.4 %reduce-scatter.5.cloned.1.call-done = bf16[192,2304]{1,0:T(8,128)(2,1)} async-done(((bf16[768,2304]{1,0:T(8,128)(2,1)}), bf16[192,2304]{1,0:T(8,128)(2,1)}) %reduce-scatter.5.cloned.1.call-update) | async-done | bytes 884752 | tf_op jit(solution)/shard_map/reduce_scatter | solution.py:257
  606.4 15.3 %all-reduce.16 = (bf16[768]{0:T(1024)(128)(2,1)S(1)}, bf16[768]{0:T(1024)(128)(2,1)S(1)}, bf16[2304]{0:T(1024)(128)(2,1)S(1)}, bf16[768]{0:T(1024)(128)(2,1)S(1)...) all-reduce(bf16[768]{0:T(1024)(128)(2,1)S(1)} %dynamic-update-slice, ...), channel_id=1, replica_groups=mesh['fsdp'=4,'ctx'=8] {'fsdp'}, use_global_device_ids=true, to_apply=%add.6 | all-reduce | flops 10752 | bytes 43008
  622.3 15.3 %all-reduce.14 = (bf16[576]{0:T(1024)(128)(2,1)S(1)}, bf16[192]{0:T(256)(128)(2,1)S(1)}, bf16[768]{0:T(1024)(128)(2,1)S(1)}, bf16[192]{0:T(256)(128)(2,1)S(1)}, ...) all-reduce(bf16[576]{0:T(1024)(128)(2,1)S(1)} %dynamic-slice.8, ...), channel_id=1, replica_groups=mesh['fsdp'=4,'ctx'=8] {'ctx'}, use_global_device_ids=true, to_apply=%region_16.17 | all-reduce | flops 2304 | bytes 9216 | tf_op jit(solution)/shard_map/psum | solution.py:293
  641.1 3.9 convolution_add_fusion.3
  647.7 45.3 %all-reduce.20.cloned.1.call-done = (bf16[192,2304]{1,0:T(8,128)(2,1)}, bf16[192,768]{1,0:T(8,128)(2,1)}, bf16[192,3072]{1,0:T(8,128)(2,1)}, bf16[768,768]{1,0:T(8,128)(2,1)}) async-done(((bf16[192,2304]{1,0:T(8,128)(2,1)}, bf16[192,768]{1,0:T(8,128)(2,1)}, bf16[192,3072]{1,0:T(8,128)(2,1)}, bf16[768,768]{1,0:T(8,128)(2,1)}), (bf16[192,2304]{1,0:T(8,128)(2,1)}, bf16[192,768]{1,0:T(8,128)(2,1)}, ...) | async-done | bytes 3538960 | tf_op jit(solution)/shard_map/psum | solution.py:292
  693.0 3.1 convert_element_type.271
  (434 shorter events, 191.8 us)
Async XLA Ops:
  7.2 52.8 %all-gather.10.cloned.1.call-start = ((), (), s32[]{:S(2)}) async-start(), calls=%async_computation.4 | async-start | bytes 4423680 | tf_op jit(solution)/shard_map/all_gather | solution.py:109
  7.9 99.8 %all-gather.12.cloned.1.call-start = ((), (), s32[]{:S(2)}) async-start(), calls=%async_computation.5 | async-start | bytes 3538944 | tf_op jit(solution)/shard_map/all_gather | solution.py:171
  33.2 31.4 %copy-start.23 = (f32[768]{0:T(1024)}, f32[768]{0:T(1024)S(1)}, u32[]{:S(2)}) copy-start(f32[768]{0:T(1024)S(1)} %convert_element_type.241) | copy-start | bytes 9220
  33.2 31.4 %copy-start.29 = (f32[768]{0:T(1024)}, f32[768]{0:T(1024)S(1)}, u32[]{:S(2)}) copy-start(f32[768]{0:T(1024)S(1)} %convert_element_type.242) | copy-start | bytes 9220
  34.7 32.3 %copy-start.27 = (f32[256,16]{0,1:T(8,128)}, f32[256,16]{0,1:T(8,128)S(1)}, u32[]{:S(2)}) copy-start(f32[256,16]{0,1:T(8,128)S(1)} %get-tuple-element.582) | copy-start | bytes 49156
  35.8 28.8 %copy-start.32 = (f32[256]{0:T(256)}, f32[256]{0:T(256)S(1)}, u32[]{:S(2)}) copy-start(f32[256]{0:T(256)S(1)} %broadcast_multiply_fusion.1) | copy-start | bytes 3076
  37.1 27.6 %copy-start.40 = (f32[256]{0:T(256)}, f32[256]{0:T(256)S(1)}, u32[]{:S(2)}) copy-start(f32[256]{0:T(256)S(1)} %fusion.73) | copy-start | bytes 3076
  37.1 27.6 %copy-start.35 = (f32[256]{0:T(256)}, f32[256]{0:T(256)S(1)}, u32[]{:S(2)}) copy-start(f32[256]{0:T(256)S(1)} %fusion.108) | copy-start | bytes 3076
  68.4 80.7 %all-gather.20.cloned.1.call-start = ((), (), s32[]{:S(2)}) async-start(), calls=%async_computation.13 | async-start | bytes 3538944 | tf_op jit(solution)/shard_map/all_gather | solution.py:172
  69.2 145.9 %all-gather.16.cloned.1.call-start = ((), (), s32[]{:S(2)}) async-start(), calls=%async_computation.7 | async-start | bytes 5898240 | tf_op jit(solution)/shard_map/all_gather | solution.py:113
  69.8 195.1 %all-gather.18.cloned.1.call-start = ((), (), s32[]{:S(2)}) async-start(), calls=%async_computation.8 | async-start | bytes 5898240 | tf_op jit(solution)/shard_map/all_gather | solution.py:115
  70.4 223.9 %all-gather.14.cloned.1.call-start = ((), (), s32[]{:S(2)}) async-start(), calls=%async_computation.6 | async-start | bytes 1474560 | tf_op jit(solution)/shard_map/all_gather | solution.py:111
  71.0 499.0 %reduce-scatter.7.cloned.1.call-start = ((), (), s32[]{:S(2)}) async-start(), calls=%async_computation.10 | async-start | bytes 1474560 | tf_op jit(solution)/shard_map/reduce_scatter | solution.py:263
  84.5 187.2 %copy-start.25 = (f32[768]{0:T(1024)}, f32[768]{0:T(1024)S(1)}, u32[]{:S(2)}) copy-start(f32[768]{0:T(1024)S(1)} %convert_element_type.250) | copy-start | bytes 9220
  149.1 64.3 %copy-start.4 = (bf16[1,256,768]{2,1,0:T(8,128)(2,1)S(1)}, bf16[1,256,768]{2,1,0:T(8,128)(2,1)}, u32[]{:S(2)}) copy-start(bf16[1,256,768]{2,1,0:T(8,128)(2,1)} %param.33) | copy-start | bytes 1179652
  158.9 4.9 copy-start
  174.7 5.7 copy-start
  191.3 4.9 copy-start
  207.0 4.8 copy-start
  213.2 13.5 %copy-start.17 = (f32[12,256]{1,0:T(8,128)}, f32[12,256]{1,0:T(8,128)S(1)}, u32[]{:S(2)}) copy-start(f32[12,256]{1,0:T(8,128)S(1)} %get-tuple-element.380) | copy-start | bytes 36868
  213.3 13.4 %copy-start.8 = (bf16[256,12,64]{0,2,1:T(8,128)(2,1)}, bf16[256,12,64]{0,2,1:T(8,128)(2,1)S(1)}, u32[]{:S(2)}) copy-start(bf16[256,12,64]{0,2,1:T(8,128)(2,1)S(1)} %fusion.99) | copy-start | bytes 1179652
  214.9 355.1 %reduce-scatter.9.cloned.1.call-start = ((), (), s32[]{:S(2)}) async-start(), calls=%async_computation.11 | async-start | bytes 5898240 | tf_op jit(solution)/shard_map/reduce_scatter | solution.py:269
  226.7 74.0 %copy-start.10 = (bf16[256,3072]{1,0:T(8,128)(2,1)}, bf16[256,3072]{1,0:T(8,128)(2,1)S(1)}, u32[]{:S(2)}) copy-start(bf16[256,3072]{1,0:T(8,128)(2,1)S(1)} %get-tuple-element.560) | copy-start | bytes 4718596
  276.6 293.4 %reduce-scatter.11.cloned.1.call-start = ((), (), s32[]{:S(2)}) async-start(), calls=%async_computation.12 | async-start | bytes 5898240 | tf_op jit(solution)/shard_map/reduce_scatter | solution.py:275
  304.3 300.2 %reduce-scatter.5.cloned.1.call-start = ((), (), s32[]{:S(2)}) async-start(), calls=%async_computation.9 | async-start | bytes 4423680 | tf_op jit(solution)/shard_map/reduce_scatter | solution.py:257
  307.7 247.0 %copy-start.28 = (f32[256,16]{0,1:T(8,128)S(1)}, f32[256,16]{0,1:T(8,128)}, u32[]{:S(2)}) copy-start(f32[256,16]{0,1:T(8,128)} %copy-done.27) | copy-start | bytes 49156
  316.4 5.8 copy-start.1
  316.4 9.3 %collective-permute-start.2 = (bf16[256,12,64]{0,2,1:T(8,128)(2,1)}, bf16[256,12,64]{0,2,1:T(8,128)(2,1)}, u32[]{:S(2)}, u32[]{:S(2)}) collective-permute-start(bf16[256,12,64]{0,2,1:T(8,128)(2,1)} %fusion.189), channel_id=1, source_target_pairs={{0,1},{1,2},{2,3},{3,4},{4,5},{5,6},{6,7},{7,0},{8,9},{9,10},{10,1... | collective-permute-start | bytes 1179656 | tf_op jit(solution)/shard_map/while/body/eval_jaxpr/ppermute | solution.py:15
  319.0 10.9 %collective-permute-start.3 = (bf16[256,12,64]{0,2,1:T(8,128)(2,1)}, bf16[256,12,64]{0,2,1:T(8,128)(2,1)}, u32[]{:S(2)}, u32[]{:S(2)}) collective-permute-start(bf16[256,12,64]{0,2,1:T(8,128)(2,1)} %fusion.190), channel_id=1, source_target_pairs={{0,1},{1,2},{2,3},{3,4},{4,5},{5,6},{6,7},{7,0},{8,9},{9,10},{10,1... | collective-permute-start | bytes 1179656 | tf_op jit(solution)/shard_map/while/body/eval_jaxpr/ppermute | solution.py:15
  320.5 13.6 %collective-permute-start = (bf16[256,12,64]{0,2,1:T(8,128)(2,1)S(1)}, bf16[256,12,64]{0,2,1:T(8,128)(2,1)}, u32[]{:S(2)}, u32[]{:S(2)}) collective-permute-start(bf16[256,12,64]{0,2,1:T(8,128)(2,1)S(1)} %copy.76), channel_id=1, source_target_pairs={{0,1},{1,2},{2,3},{3,4},{4,5},{5,6},{6,7},{7,0},{8,9},{9,10},{10,1... | collective-permute-start | bytes 1179656 | tf_op jit(solution)/shard_map/while/body/eval_jaxpr/ppermute | solution.py:15
  320.6 17.7 %collective-permute-start.1 = (bf16[256,12,64]{0,2,1:T(8,128)(2,1)}, bf16[256,12,64]{0,2,1:T(8,128)(2,1)}, u32[]{:S(2)}, u32[]{:S(2)}) collective-permute-start(bf16[256,12,64]{0,2,1:T(8,128)(2,1)} %copy.77), channel_id=1, source_target_pairs={{0,1},{1,2},{2,3},{3,4},{4,5},{5,6},{6,7},{7,0},{8,9},{9,10},{10,1... | collective-permute-start | bytes 1179656 | tf_op jit(solution)/shard_map/while/body/eval_jaxpr/ppermute | solution.py:15
  346.9 9.3 %collective-permute-start.2 = (bf16[256,12,64]{0,2,1:T(8,128)(2,1)}, bf16[256,12,64]{0,2,1:T(8,128)(2,1)}, u32[]{:S(2)}, u32[]{:S(2)}) collective-permute-start(bf16[256,12,64]{0,2,1:T(8,128)(2,1)} %fusion.189), channel_id=1, source_target_pairs={{0,1},{1,2},{2,3},{3,4},{4,5},{5,6},{6,7},{7,0},{8,9},{9,10},{10,1... | collective-permute-start | bytes 1179656 | tf_op jit(solution)/shard_map/while/body/eval_jaxpr/ppermute | solution.py:15
  349.6 10.9 %collective-permute-start.3 = (bf16[256,12,64]{0,2,1:T(8,128)(2,1)}, bf16[256,12,64]{0,2,1:T(8,128)(2,1)}, u32[]{:S(2)}, u32[]{:S(2)}) collective-permute-start(bf16[256,12,64]{0,2,1:T(8,128)(2,1)} %fusion.190), channel_id=1, source_target_pairs={{0,1},{1,2},{2,3},{3,4},{4,5},{5,6},{6,7},{7,0},{8,9},{9,10},{10,1... | collective-permute-start | bytes 1179656 | tf_op jit(solution)/shard_map/while/body/eval_jaxpr/ppermute | solution.py:15
  349.6 15.1 %collective-permute-start = (bf16[256,12,64]{0,2,1:T(8,128)(2,1)S(1)}, bf16[256,12,64]{0,2,1:T(8,128)(2,1)}, u32[]{:S(2)}, u32[]{:S(2)}) collective-permute-start(bf16[256,12,64]{0,2,1:T(8,128)(2,1)S(1)} %copy.76), channel_id=1, source_target_pairs={{0,1},{1,2},{2,3},{3,4},{4,5},{5,6},{6,7},{7,0},{8,9},{9,10},{10,1... | collective-permute-start | bytes 1179656 | tf_op jit(solution)/shard_map/while/body/eval_jaxpr/ppermute | solution.py:15
  349.6 19.3 %collective-permute-start.1 = (bf16[256,12,64]{0,2,1:T(8,128)(2,1)}, bf16[256,12,64]{0,2,1:T(8,128)(2,1)}, u32[]{:S(2)}, u32[]{:S(2)}) collective-permute-start(bf16[256,12,64]{0,2,1:T(8,128)(2,1)} %copy.77), channel_id=1, source_target_pairs={{0,1},{1,2},{2,3},{3,4},{4,5},{5,6},{6,7},{7,0},{8,9},{9,10},{10,1... | collective-permute-start | bytes 1179656 | tf_op jit(solution)/shard_map/while/body/eval_jaxpr/ppermute | solution.py:15
  377.6 9.3 %collective-permute-start.2 = (bf16[256,12,64]{0,2,1:T(8,128)(2,1)}, bf16[256,12,64]{0,2,1:T(8,128)(2,1)}, u32[]{:S(2)}, u32[]{:S(2)}) collective-permute-start(bf16[256,12,64]{0,2,1:T(8,128)(2,1)} %fusion.189), channel_id=1, source_target_pairs={{0,1},{1,2},{2,3},{3,4},{4,5},{5,6},{6,7},{7,0},{8,9},{9,10},{10,1... | collective-permute-start | bytes 1179656 | tf_op jit(solution)/shard_map/while/body/eval_jaxpr/ppermute | solution.py:15
  380.3 10.9 %collective-permute-start.3 = (bf16[256,12,64]{0,2,1:T(8,128)(2,1)}, bf16[256,12,64]{0,2,1:T(8,128)(2,1)}, u32[]{:S(2)}, u32[]{:S(2)}) collective-permute-start(bf16[256,12,64]{0,2,1:T(8,128)(2,1)} %fusion.190), channel_id=1, source_target_pairs={{0,1},{1,2},{2,3},{3,4},{4,5},{5,6},{6,7},{7,0},{8,9},{9,10},{10,1... | collective-permute-start | bytes 1179656 | tf_op jit(solution)/shard_map/while/body/eval_jaxpr/ppermute | solution.py:15
  380.3 15.1 %collective-permute-start = (bf16[256,12,64]{0,2,1:T(8,128)(2,1)S(1)}, bf16[256,12,64]{0,2,1:T(8,128)(2,1)}, u32[]{:S(2)}, u32[]{:S(2)}) collective-permute-start(bf16[256,12,64]{0,2,1:T(8,128)(2,1)S(1)} %copy.76), channel_id=1, source_target_pairs={{0,1},{1,2},{2,3},{3,4},{4,5},{5,6},{6,7},{7,0},{8,9},{9,10},{10,1... | collective-permute-start | bytes 1179656 | tf_op jit(solution)/shard_map/while/body/eval_jaxpr/ppermute | solution.py:15
  380.3 19.3 %collective-permute-start.1 = (bf16[256,12,64]{0,2,1:T(8,128)(2,1)}, bf16[256,12,64]{0,2,1:T(8,128)(2,1)}, u32[]{:S(2)}, u32[]{:S(2)}) collective-permute-start(bf16[256,12,64]{0,2,1:T(8,128)(2,1)} %copy.77), channel_id=1, source_target_pairs={{0,1},{1,2},{2,3},{3,4},{4,5},{5,6},{6,7},{7,0},{8,9},{9,10},{10,1... | collective-permute-start | bytes 1179656 | tf_op jit(solution)/shard_map/while/body/eval_jaxpr/ppermute | solution.py:15
  408.2 9.3 %collective-permute-start.2 = (bf16[256,12,64]{0,2,1:T(8,128)(2,1)}, bf16[256,12,64]{0,2,1:T(8,128)(2,1)}, u32[]{:S(2)}, u32[]{:S(2)}) collective-permute-start(bf16[256,12,64]{0,2,1:T(8,128)(2,1)} %fusion.189), channel_id=1, source_target_pairs={{0,1},{1,2},{2,3},{3,4},{4,5},{5,6},{6,7},{7,0},{8,9},{9,10},{10,1... | collective-permute-start | bytes 1179656 | tf_op jit(solution)/shard_map/while/body/eval_jaxpr/ppermute | solution.py:15
  410.9 10.8 %collective-permute-start.3 = (bf16[256,12,64]{0,2,1:T(8,128)(2,1)}, bf16[256,12,64]{0,2,1:T(8,128)(2,1)}, u32[]{:S(2)}, u32[]{:S(2)}) collective-permute-start(bf16[256,12,64]{0,2,1:T(8,128)(2,1)} %fusion.190), channel_id=1, source_target_pairs={{0,1},{1,2},{2,3},{3,4},{4,5},{5,6},{6,7},{7,0},{8,9},{9,10},{10,1... | collective-permute-start | bytes 1179656 | tf_op jit(solution)/shard_map/while/body/eval_jaxpr/ppermute | solution.py:15
  410.9 15.0 %collective-permute-start = (bf16[256,12,64]{0,2,1:T(8,128)(2,1)S(1)}, bf16[256,12,64]{0,2,1:T(8,128)(2,1)}, u32[]{:S(2)}, u32[]{:S(2)}) collective-permute-start(bf16[256,12,64]{0,2,1:T(8,128)(2,1)S(1)} %copy.76), channel_id=1, source_target_pairs={{0,1},{1,2},{2,3},{3,4},{4,5},{5,6},{6,7},{7,0},{8,9},{9,10},{10,1... | collective-permute-start | bytes 1179656 | tf_op jit(solution)/shard_map/while/body/eval_jaxpr/ppermute | solution.py:15
  410.9 19.2 %collective-permute-start.1 = (bf16[256,12,64]{0,2,1:T(8,128)(2,1)}, bf16[256,12,64]{0,2,1:T(8,128)(2,1)}, u32[]{:S(2)}, u32[]{:S(2)}) collective-permute-start(bf16[256,12,64]{0,2,1:T(8,128)(2,1)} %copy.77), channel_id=1, source_target_pairs={{0,1},{1,2},{2,3},{3,4},{4,5},{5,6},{6,7},{7,0},{8,9},{9,10},{10,1... | collective-permute-start | bytes 1179656 | tf_op jit(solution)/shard_map/while/body/eval_jaxpr/ppermute | solution.py:15
  438.8 9.3 %collective-permute-start.2 = (bf16[256,12,64]{0,2,1:T(8,128)(2,1)}, bf16[256,12,64]{0,2,1:T(8,128)(2,1)}, u32[]{:S(2)}, u32[]{:S(2)}) collective-permute-start(bf16[256,12,64]{0,2,1:T(8,128)(2,1)} %fusion.189), channel_id=1, source_target_pairs={{0,1},{1,2},{2,3},{3,4},{4,5},{5,6},{6,7},{7,0},{8,9},{9,10},{10,1... | collective-permute-start | bytes 1179656 | tf_op jit(solution)/shard_map/while/body/eval_jaxpr/ppermute | solution.py:15
  441.5 10.9 %collective-permute-start.3 = (bf16[256,12,64]{0,2,1:T(8,128)(2,1)}, bf16[256,12,64]{0,2,1:T(8,128)(2,1)}, u32[]{:S(2)}, u32[]{:S(2)}) collective-permute-start(bf16[256,12,64]{0,2,1:T(8,128)(2,1)} %fusion.190), channel_id=1, source_target_pairs={{0,1},{1,2},{2,3},{3,4},{4,5},{5,6},{6,7},{7,0},{8,9},{9,10},{10,1... | collective-permute-start | bytes 1179656 | tf_op jit(solution)/shard_map/while/body/eval_jaxpr/ppermute | solution.py:15
  441.5 15.1 %collective-permute-start = (bf16[256,12,64]{0,2,1:T(8,128)(2,1)S(1)}, bf16[256,12,64]{0,2,1:T(8,128)(2,1)}, u32[]{:S(2)}, u32[]{:S(2)}) collective-permute-start(bf16[256,12,64]{0,2,1:T(8,128)(2,1)S(1)} %copy.76), channel_id=1, source_target_pairs={{0,1},{1,2},{2,3},{3,4},{4,5},{5,6},{6,7},{7,0},{8,9},{9,10},{10,1... | collective-permute-start | bytes 1179656 | tf_op jit(solution)/shard_map/while/body/eval_jaxpr/ppermute | solution.py:15
  441.5 19.3 %collective-permute-start.1 = (bf16[256,12,64]{0,2,1:T(8,128)(2,1)}, bf16[256,12,64]{0,2,1:T(8,128)(2,1)}, u32[]{:S(2)}, u32[]{:S(2)}) collective-permute-start(bf16[256,12,64]{0,2,1:T(8,128)(2,1)} %copy.77), channel_id=1, source_target_pairs={{0,1},{1,2},{2,3},{3,4},{4,5},{5,6},{6,7},{7,0},{8,9},{9,10},{10,1... | collective-permute-start | bytes 1179656 | tf_op jit(solution)/shard_map/while/body/eval_jaxpr/ppermute | solution.py:15
  469.4 9.3 %collective-permute-start.2 = (bf16[256,12,64]{0,2,1:T(8,128)(2,1)}, bf16[256,12,64]{0,2,1:T(8,128)(2,1)}, u32[]{:S(2)}, u32[]{:S(2)}) collective-permute-start(bf16[256,12,64]{0,2,1:T(8,128)(2,1)} %fusion.189), channel_id=1, source_target_pairs={{0,1},{1,2},{2,3},{3,4},{4,5},{5,6},{6,7},{7,0},{8,9},{9,10},{10,1... | collective-permute-start | bytes 1179656 | tf_op jit(solution)/shard_map/while/body/eval_jaxpr/ppermute | solution.py:15
  472.0 10.9 %collective-permute-start.3 = (bf16[256,12,64]{0,2,1:T(8,128)(2,1)}, bf16[256,12,64]{0,2,1:T(8,128)(2,1)}, u32[]{:S(2)}, u32[]{:S(2)}) collective-permute-start(bf16[256,12,64]{0,2,1:T(8,128)(2,1)} %fusion.190), channel_id=1, source_target_pairs={{0,1},{1,2},{2,3},{3,4},{4,5},{5,6},{6,7},{7,0},{8,9},{9,10},{10,1... | collective-permute-start | bytes 1179656 | tf_op jit(solution)/shard_map/while/body/eval_jaxpr/ppermute | solution.py:15
  472.0 15.1 %collective-permute-start = (bf16[256,12,64]{0,2,1:T(8,128)(2,1)S(1)}, bf16[256,12,64]{0,2,1:T(8,128)(2,1)}, u32[]{:S(2)}, u32[]{:S(2)}) collective-permute-start(bf16[256,12,64]{0,2,1:T(8,128)(2,1)S(1)} %copy.76), channel_id=1, source_target_pairs={{0,1},{1,2},{2,3},{3,4},{4,5},{5,6},{6,7},{7,0},{8,9},{9,10},{10,1... | collective-permute-start | bytes 1179656 | tf_op jit(solution)/shard_map/while/body/eval_jaxpr/ppermute | solution.py:15
  472.0 19.3 %collective-permute-start.1 = (bf16[256,12,64]{0,2,1:T(8,128)(2,1)}, bf16[256,12,64]{0,2,1:T(8,128)(2,1)}, u32[]{:S(2)}, u32[]{:S(2)}) collective-permute-start(bf16[256,12,64]{0,2,1:T(8,128)(2,1)} %copy.77), channel_id=1, source_target_pairs={{0,1},{1,2},{2,3},{3,4},{4,5},{5,6},{6,7},{7,0},{8,9},{9,10},{10,1... | collective-permute-start | bytes 1179656 | tf_op jit(solution)/shard_map/while/body/eval_jaxpr/ppermute | solution.py:15
  499.9 9.3 %collective-permute-start.2 = (bf16[256,12,64]{0,2,1:T(8,128)(2,1)}, bf16[256,12,64]{0,2,1:T(8,128)(2,1)}, u32[]{:S(2)}, u32[]{:S(2)}) collective-permute-start(bf16[256,12,64]{0,2,1:T(8,128)(2,1)} %fusion.189), channel_id=1, source_target_pairs={{0,1},{1,2},{2,3},{3,4},{4,5},{5,6},{6,7},{7,0},{8,9},{9,10},{10,1... | collective-permute-start | bytes 1179656 | tf_op jit(solution)/shard_map/while/body/eval_jaxpr/ppermute | solution.py:15
  502.6 10.9 %collective-permute-start.3 = (bf16[256,12,64]{0,2,1:T(8,128)(2,1)}, bf16[256,12,64]{0,2,1:T(8,128)(2,1)}, u32[]{:S(2)}, u32[]{:S(2)}) collective-permute-start(bf16[256,12,64]{0,2,1:T(8,128)(2,1)} %fusion.190), channel_id=1, source_target_pairs={{0,1},{1,2},{2,3},{3,4},{4,5},{5,6},{6,7},{7,0},{8,9},{9,10},{10,1... | collective-permute-start | bytes 1179656 | tf_op jit(solution)/shard_map/while/body/eval_jaxpr/ppermute | solution.py:15
  502.6 15.1 %collective-permute-start = (bf16[256,12,64]{0,2,1:T(8,128)(2,1)S(1)}, bf16[256,12,64]{0,2,1:T(8,128)(2,1)}, u32[]{:S(2)}, u32[]{:S(2)}) collective-permute-start(bf16[256,12,64]{0,2,1:T(8,128)(2,1)S(1)} %copy.76), channel_id=1, source_target_pairs={{0,1},{1,2},{2,3},{3,4},{4,5},{5,6},{6,7},{7,0},{8,9},{9,10},{10,1... | collective-permute-start | bytes 1179656 | tf_op jit(solution)/shard_map/while/body/eval_jaxpr/ppermute | solution.py:15
  502.6 19.3 %collective-permute-start.1 = (bf16[256,12,64]{0,2,1:T(8,128)(2,1)}, bf16[256,12,64]{0,2,1:T(8,128)(2,1)}, u32[]{:S(2)}, u32[]{:S(2)}) collective-permute-start(bf16[256,12,64]{0,2,1:T(8,128)(2,1)} %copy.77), channel_id=1, source_target_pairs={{0,1},{1,2},{2,3},{3,4},{4,5},{5,6},{6,7},{7,0},{8,9},{9,10},{10,1... | collective-permute-start | bytes 1179656 | tf_op jit(solution)/shard_map/while/body/eval_jaxpr/ppermute | solution.py:15
  530.5 9.3 %collective-permute-start.2 = (bf16[256,12,64]{0,2,1:T(8,128)(2,1)}, bf16[256,12,64]{0,2,1:T(8,128)(2,1)}, u32[]{:S(2)}, u32[]{:S(2)}) collective-permute-start(bf16[256,12,64]{0,2,1:T(8,128)(2,1)} %fusion.189), channel_id=1, source_target_pairs={{0,1},{1,2},{2,3},{3,4},{4,5},{5,6},{6,7},{7,0},{8,9},{9,10},{10,1... | collective-permute-start | bytes 1179656 | tf_op jit(solution)/shard_map/while/body/eval_jaxpr/ppermute | solution.py:15
  533.1 10.9 %collective-permute-start.3 = (bf16[256,12,64]{0,2,1:T(8,128)(2,1)}, bf16[256,12,64]{0,2,1:T(8,128)(2,1)}, u32[]{:S(2)}, u32[]{:S(2)}) collective-permute-start(bf16[256,12,64]{0,2,1:T(8,128)(2,1)} %fusion.190), channel_id=1, source_target_pairs={{0,1},{1,2},{2,3},{3,4},{4,5},{5,6},{6,7},{7,0},{8,9},{9,10},{10,1... | collective-permute-start | bytes 1179656 | tf_op jit(solution)/shard_map/while/body/eval_jaxpr/ppermute | solution.py:15
  533.1 15.1 %collective-permute-start = (bf16[256,12,64]{0,2,1:T(8,128)(2,1)S(1)}, bf16[256,12,64]{0,2,1:T(8,128)(2,1)}, u32[]{:S(2)}, u32[]{:S(2)}) collective-permute-start(bf16[256,12,64]{0,2,1:T(8,128)(2,1)S(1)} %copy.76), channel_id=1, source_target_pairs={{0,1},{1,2},{2,3},{3,4},{4,5},{5,6},{6,7},{7,0},{8,9},{9,10},{10,1... | collective-permute-start | bytes 1179656 | tf_op jit(solution)/shard_map/while/body/eval_jaxpr/ppermute | solution.py:15
  533.1 19.3 %collective-permute-start.1 = (bf16[256,12,64]{0,2,1:T(8,128)(2,1)}, bf16[256,12,64]{0,2,1:T(8,128)(2,1)}, u32[]{:S(2)}, u32[]{:S(2)}) collective-permute-start(bf16[256,12,64]{0,2,1:T(8,128)(2,1)} %copy.77), channel_id=1, source_target_pairs={{0,1},{1,2},{2,3},{3,4},{4,5},{5,6},{6,7},{7,0},{8,9},{9,10},{10,1... | collective-permute-start | bytes 1179656 | tf_op jit(solution)/shard_map/while/body/eval_jaxpr/ppermute | solution.py:15
  559.5 133.5 %all-reduce.20.cloned.1.call-start = ((), (), s32[]{:S(2)}) async-start(), calls=%async_computation.14 | async-start | bytes 7077888 | tf_op jit(solution)/shard_map/psum | solution.py:292
  563.0 4.8 copy-start.44
  569.9 36.5 %copy-start.42 = (bf16[3072]{0:T(1024)(128)(2,1)S(1)}, bf16[3072]{0:T(1024)(128)(2,1)}, u32[]{:S(2)}) copy-start(bf16[3072]{0:T(1024)(128)(2,1)} %get-tuple-element.586) | copy-start | bytes 18436
  569.9 71.1 %copy-start.11 = (bf16[256,3072]{1,0:T(8,128)(2,1)S(1)}, bf16[256,3072]{1,0:T(8,128)(2,1)}, u32[]{:S(2)}) copy-start(bf16[256,3072]{1,0:T(8,128)(2,1)} %copy-done.10) | copy-start | bytes 4718596
  638.8 61.1 %copy-start.43 = (f32[192]{0:T(256)}, f32[192]{0:T(256)S(1)}, u32[]{:S(2)}) copy-start(f32[192]{0:T(256)S(1)} %convert_element_type.269) | copy-start | bytes 2308
  (64 other events, 133.2 us)
Sparse Core Ops, SparseCore 0:
  9.9 50.0 all-gather.9
  68.5 39.1 all-gather.11
  109.9 39.1 all-gather.19
  150.8 55.2 all-gather.15
  207.8 57.0 all-gather.17
  266.6 27.7 all-gather.13
  297.3 28.5 reduce-scatter.6
  328.8 57.0 reduce-scatter.8
  388.9 57.0 reduce-scatter.10
  559.6 44.8 reduce-scatter.4
  607.1 85.8 all-reduce.19
where the time goes:
time: 711 us; the launch traced here: 707 us
  waiting for transfers between devices  329 us (46%)
  matrix products  151 us (21%)
  blocking collectives  69.9 us (10%)
  other arithmetic  63.4 us (9%)
  local copies, waits for them, and re-layouts  62.1 us (9%)
  between operations  17.8 us (3%)
  loops' own time  8.68 us (1%)
    ppermute x32, waiting for transfers between devices, from_behind(): return lax.ppermute(x, axis, [(i, (i + by) % size) for i in range(size)])  113 us
    psum x1, waiting for transfers between devices, on_device(): lax.psum(shares[0].astype(jnp.bfloat16), 'ctx').astype(jnp.float32)  45.3 us
    all_gather x1, waiting for transfers between devices, on_device(): value_piece = lax.all_gather(values, 'ctx', axis=0, tiled=True)  41.4 us
    all_gather x1, waiting for transfers between devices, on_device(): lax.all_gather(down_weight, 'fsdp', axis=0, tiled=True)  38.2 us
    reduce_scatter x1, waiting for transfers between devices, on_device(): lax.psum_scatter(in_weight_part.astype(jnp.bfloat16), 'fsdp', scatter_dim...  34.4 us
    unnamed x2, blocking collectives  33.7 us
    while x108, local copies, waits for them, and re-layouts  31 us
    all_gather x1, waiting for transfers between devices, on_device(): lax.all_gather(in_weight, 'fsdp', axis=0, tiled=True)  22.8 us
  transfers between devices with their start and end apart: 43, of which 39 were waited for; matrix products, arithmetic and copies ran while one was open for 35% of the time, Pallas kernels for 0%

commit v1 on v0

--- a/solution.py
+++ b/solution.py
@@ -169,7 +169,12 @@
     )
     carry = start_state
     key_piece = lax.all_gather(keys, "ctx", axis=0, tiled=True)
-    value_piece = lax.all_gather(values, "ctx", axis=0, tiled=True)
+    ring = [values]
+    for hop in range(7):
+        ring.append(lax.ppermute(ring[-1], "ctx", [(dev, (dev + 1) % 8) for dev in range(8)]))
+    value_piece = jnp.roll(
+        jnp.concatenate(ring[::-1], axis=0), (lax.axis_index("ctx") + 1) * ring[0].shape[0], axis=0
+    )
     count = key_piece.shape[0]
     size = 512
 

time: 711 us -> 680 us (0.956)
  waiting for transfers between devices: 329 us -> 289 us
    ppermute x0 -> x7, waiting for transfers between devices: none -> 70.3 us  [on_device(): lax.ppermute(ring[-1], 'ctx', [(dev, (dev + 1) % 8) for dev in range(8)])]
    all_gather x1 -> x0, waiting for transfers between devices: 41.4 us -> none  [on_device(): value_piece = lax.all_gather(values, 'ctx', axis=0, tiled=True)]
    all_gather x1, waiting for transfers between devices: 38.2 us -> 0.02 us  [on_device(): lax.all_gather(down_weight, 'fsdp', axis=0, tiled=True)]
    all_gather x1, waiting for transfers between devices: 17.6 us -> 0.02 us  [on_device(): lax.all_gather(out_weight, 'fsdp', axis=0, tiled=True)]
    all_gather x1, waiting for transfers between devices: 13.7 us -> 0.01 us  [on_device(): key_piece = lax.all_gather(keys, 'ctx', axis=0, tiled=True)]
    unnamed x106 -> x143, local copies, waits for them, and re-layouts: 11.4 us -> 18.6 us
  transfers between devices with their start and end apart: 43 -> 49, of which waited for: 39 -> 41; matrix products, arithmetic and copies ran while one was open for 35% -> 38% of each run, Pallas kernels for 0% -> 0%
where the time goes in v1:
time: 680 us; the launch traced here: 676 us
  waiting for transfers between devices  289 us (42%)
  matrix products  153 us (22%)
  local copies, waits for them, and re-layouts  69 us (10%)
  other arithmetic  67.2 us (10%)
  blocking collectives  66.9 us (10%)
  between operations  18.4 us (3%)
  loops' own time  8.7 us (1%)
    ppermute x32, waiting for transfers between devices, from_behind(): return lax.ppermute(x, axis, [(i, (i + by) % size) for i in range(size)])  114 us
    ppermute x7, waiting for transfers between devices, on_device(): lax.ppermute(ring[-1], 'ctx', [(dev, (dev + 1) % 8) for dev in range(8)])  70.3 us
    psum x1, waiting for transfers between devices, on_device(): lax.psum(shares[0].astype(jnp.bfloat16), 'ctx').astype(jnp.float32)  45.1 us
    reduce_scatter x1, waiting for transfers between devices, on_device(): lax.psum_scatter(in_weight_part.astype(jnp.bfloat16), 'fsdp', scatter_dim...  34.4 us
    unnamed x2, blocking collectives  33.7 us
    while x108, local copies, waits for them, and re-layouts  30.5 us
    all_gather x1, waiting for transfers between devices, on_device(): lax.all_gather(in_weight, 'fsdp', axis=0, tiled=True)  22.8 us
    dot_general x4, matrix products, softmax_step(): jnp.einsum('qhd,khd->hqk', queries, keys, preferred_element_type=jnp.floa...  22 us
  transfers between devices with their start and end apart: 49, of which 41 were waited for; matrix products, arithmetic and copies ran while one was open for 38% of the time, Pallas kernels for 0%

profile of v1, /device:TPU:0, one launch (start us, length us, event | category | flops | bytes accessed | tf_op | source)
XLA Modules:
  0.0 675.8 jit_solution(13908686526716915741)
XLA Ops:
  14.8 18.4 %all-reduce.17 = (bf16[768]{0:T(1024)(128)(2,1)}, bf16[768]{0:T(1024)(128)(2,1)}, bf16[2304]{0:T(1024)(128)(2,1)S(1)}, bf16[768]{0:T(1024)(128)(2,1)S(1)}, bf16[768]{0:T(1024)(128)(2,1)S(1)}) all-reduce(bf16[768]{0:T(1024)(128)(2,1)S(1)} %dynamic-update-slice.5, ...), channel_id=1, replica_groups=mesh['fsdp'=4,'ctx'=8] {'fsdp'}, use_global_device_ids=true, to_apply=%add.5 | all-reduce | flops 5376 | bytes 21504
  37.1 22.8 %all-gather.8.cloned.1.call-done = bf16[768,2304]{1,0:T(8,128)(2,1)} async-done(((bf16[192,2304]{1,0:T(8,128)(2,1)}), bf16[768,2304]{1,0:T(8,128)(2,1)}) %all-gather.8.cloned.1.call-update) | async-done | bytes 3538960 | tf_op jit(solution)/shard_map/all_gather | solution.py:109
  59.9 4.7 convolution_add_fusion
  70.7 9.3 %collective-permute-done.4 = bf16[256,12,64]{0,2,1:T(8,128)(2,1)S(1)} collective-permute-done((bf16[256,12,64]{0,2,1:T(8,128)(2,1)}, bf16[256,12,64]{0,2,1:T(8,128)(2,1)S(1)}, u32[]{:S(2)}, u32[]{:S(2)}) %collective-permute-start.4) | collective-permute-done | bytes 393248 | tf_op jit(solution)/shard_map/ppermute | solution.py:174
  80.0 17.3 %collective-permute-done.5 = bf16[256,12,64]{0,2,1:T(8,128)(2,1)S(1)} collective-permute-done((bf16[256,12,64]{0,2,1:T(8,128)(2,1)S(1)}, bf16[256,12,64]{0,2,1:T(8,128)(2,1)S(1)}, u32[]{:S(2)}, u32[]{:S(2)}) %collective-permute-start.5) | collective-permute-done | bytes 393248 | tf_op jit(solution)/shard_map/ppermute | solution.py:174
  98.0 16.6 %collective-permute-done.6 = bf16[256,12,64]{0,2,1:T(8,128)(2,1)S(1)} collective-permute-done((bf16[256,12,64]{0,2,1:T(8,128)(2,1)S(1)}, bf16[256,12,64]{0,2,1:T(8,128)(2,1)S(1)}, u32[]{:S(2)}, u32[]{:S(2)}) %collective-permute-start.6) | collective-permute-done | bytes 393248 | tf_op jit(solution)/shard_map/ppermute | solution.py:174
  115.3 9.0 %collective-permute-done.7 = bf16[256,12,64]{0,2,1:T(8,128)(2,1)S(1)} collective-permute-done((bf16[256,12,64]{0,2,1:T(8,128)(2,1)S(1)}, bf16[256,12,64]{0,2,1:T(8,128)(2,1)S(1)}, u32[]{:S(2)}, u32[]{:S(2)}) %collective-permute-start.7) | collective-permute-done | bytes 393248 | tf_op jit(solution)/shard_map/ppermute | solution.py:174
  125.1 9.0 %collective-permute-done.8 = bf16[256,12,64]{0,2,1:T(8,128)(2,1)S(1)} collective-permute-done((bf16[256,12,64]{0,2,1:T(8,128)(2,1)S(1)}, bf16[256,12,64]{0,2,1:T(8,128)(2,1)S(1)}, u32[]{:S(2)}, u32[]{:S(2)}) %collective-permute-start.8) | collective-permute-done | bytes 393248 | tf_op jit(solution)/shard_map/ppermute | solution.py:174
  134.8 9.1 %collective-permute-done.9 = bf16[256,12,64]{0,2,1:T(8,128)(2,1)} collective-permute-done((bf16[256,12,64]{0,2,1:T(8,128)(2,1)S(1)}, bf16[256,12,64]{0,2,1:T(8,128)(2,1)}, u32[]{:S(2)}, u32[]{:S(2)}) %collective-permute-start.9) | collective-permute-done | bytes 393248 | tf_op jit(solution)/shard_map/ppermute | solution.py:174
  147.2 8.2 %all-gather.1 = bf16[4,1,768]{2,1,0:T(2,128)(2,1)S(1)} all-gather(bf16[1,1,768]{2,1,0:T(2,128)(2,1)S(1)} %reshape.292), channel_id=1, replica_groups=mesh['fsdp'=4,'ctx'=8] {'fsdp'}, dimensions={0}, use_global_device_ids=true | all-gather | bytes 7680 | tf_op jit(solution)/shard_map/all_gather | solution.py:114
  156.1 9.6 %all-gather = s32[1,2048]{1,0:T(1,128)} all-gather(s32[1,256]{1,0:T(1,128)} %param.20), channel_id=2, replica_groups=mesh['fsdp'=4,'ctx'=8] {'ctx'}, dimensions={1}, use_global_device_ids=true | all-gather | bytes 9216 | tf_op jit(solution)/shard_map/all_gather | solution.py:141
  174.3 64.2 %while.39 = (s32[]{:T(128)}, f32[12,256]{1,0:T(8,128)S(1)}, f32[12,256]{1,0:T(8,128)S(1)}, f32[256,12,64]{0,2,1:T(8,128)S(1)}, s32[4]{0:T(128)S(1)}, /*index=5*/...) while((s32[]{:T(128)}, f32[12,256]{1,0:T(8,128)S(1)}, ...), condition=%wide.region_5.6_spmd.clone, body=%wide.region_2.5_spmd.clone.sunk | while | flops 420694016 | bytes 48307420 | solution.py:188
  178.5 5.5 fusion.174
  184.0 5.6 fusion.178
  195.2 5.5 fusion.174
  200.8 4.8 fusion.178
  211.1 5.5 fusion.174
  216.6 4.8 fusion.178
  226.9 5.5 fusion.174
  232.4 4.7 fusion.178
  240.6 11.4 %multiply_convert_fusion.1 = (bf16[256,3072]{1,0:T(8,128)(2,1)S(1)}, f32[256,3072]{1,0:T(8,128)}, f32[256,3072]{1,0:T(8,128)}) fusion(f32[3072]{0:T(1024)S(1)} %bitcast.236, bf16[768,3072]{1,0:T(8,128)(2,1)} %all-gather.14.cloned.1.call-done, bf16[1,256,768]{2,1,0:T(8,128)(2,1)S(1)} %copy-done.3, f32[768]{0:T(1024)S(1)} %copy-done.40, ...), kind=kOutput, calls=%fused_computation.54 | convolution fusion | flops 1261043712 | bytes 12996608 | tf_op jit(solution)/shard_map/dot_general | solution.py:193
  252.0 7.6 %fusion.120 = (bf16[3072]{0:T(1024)(128)(2,1)}, bf16[256,3072]{1,0:T(8,128)(2,1)S(1)}) fusion(f32[256,3072]{1,0:T(8,128)} %get-tuple-element.561, f32[256,3072]{1,0:T(8,128)} %get-tuple-element.585, bf16[3072,768]{1,0:T(8,128)(2,1)} %all-gather.16.cloned.1.call-done, bf16[1,256,768]{2,1,0:T(8,128)(2,1)S(1)} %copy-done.4), kind=kOutput, calls=%fused_computation.190 | convolution fusion | flops 1219752960 | bytes 12982272 | tf_op jit(solution)/shard_map/dot_general | solution.py:47
  260.7 3.7 convolution_convert_fusion.1
  269.0 3.6 convolution_convert_fusion
  276.0 245.1 %while.40 = (s32[]{:T(128)}, bf16[256,12,64]{0,2,1:T(8,128)(2,1)}, bf16[256,12,64]{0,2,1:T(8,128)(2,1)}, f32[256,12,64]{0,2,1:T(8,128)S(1)}, f32[256,12,64]{0,2,...) while((s32[]{:T(128)}, bf16[256,12,64]{0,2,1:T(8,128)(2,1)}, ...), condition=%wide.region_9.10_spmd.clone, body=%wide.region_8.9_spmd.clone.sunk | while | flops 513605632 | bytes 40837772 | solution.py:245
  291.4 2.6 collective-permute-done.2
  295.1 3.1 collective-permute-done.3
  302.5 4.2 collective-permute-done.1
  315.4 2.6 fusion.191
  320.4 4.4 collective-permute-done.2
  325.8 3.1 collective-permute-done.3
  333.2 4.2 collective-permute-done.1
  346.0 2.7 fusion.191
  350.3 5.0 collective-permute-done.2
  356.4 3.1 collective-permute-done.3
  363.8 4.2 collective-permute-done.1
  376.6 2.6 fusion.191
  380.9 5.0 collective-permute-done.2
  387.0 3.1 collective-permute-done.3
  394.4 4.2 collective-permute-done.1
  407.4 2.6 fusion.191
  411.6 5.0 collective-permute-done.2
  417.7 3.1 collective-permute-done.3
  425.1 4.2 collective-permute-done.1
  438.0 2.6 fusion.191
  442.2 5.0 collective-permute-done.2
  448.3 3.1 collective-permute-done.3
  455.7 4.2 collective-permute-done.1
  468.6 2.6 fusion.191
  472.8 5.0 collective-permute-done.2
  478.9 3.1 collective-permute-done.3
  486.3 4.2 collective-permute-done.1
  499.2 2.6 fusion.191
  503.4 5.0 collective-permute-done.2
  509.5 3.1 collective-permute-done.3
  516.9 4.2 collective-permute-done.1
  524.9 3.2 convolution_convert_fusion.2
  531.6 4.8 fusion.122
  538.7 34.4 %reduce-scatter.5.cloned.1.call-done = bf16[192,2304]{1,0:T(8,128)(2,1)} async-done(((bf16[768,2304]{1,0:T(8,128)(2,1)}), bf16[192,2304]{1,0:T(8,128)(2,1)}) %reduce-scatter.5.cloned.1.call-update) | async-done | bytes 884752 | tf_op jit(solution)/shard_map/reduce_scatter | solution.py:262
  575.1 15.3 %all-reduce.16 = (bf16[768]{0:T(1024)(128)(2,1)S(1)}, bf16[768]{0:T(1024)(128)(2,1)S(1)}, bf16[2304]{0:T(1024)(128)(2,1)S(1)}, bf16[768]{0:T(1024)(128)(2,1)S(1)...) all-reduce(bf16[768]{0:T(1024)(128)(2,1)S(1)} %dynamic-update-slice, ...), channel_id=1, replica_groups=mesh['fsdp'=4,'ctx'=8] {'fsdp'}, use_global_device_ids=true, to_apply=%add.6 | all-reduce | flops 10752 | bytes 43008
  591.0 15.3 %all-reduce.14 = (bf16[576]{0:T(1024)(128)(2,1)S(1)}, bf16[192]{0:T(256)(128)(2,1)S(1)}, bf16[768]{0:T(1024)(128)(2,1)S(1)}, bf16[192]{0:T(256)(128)(2,1)S(1)}, ...) all-reduce(bf16[576]{0:T(1024)(128)(2,1)S(1)} %dynamic-slice.8, ...), channel_id=1, replica_groups=mesh['fsdp'=4,'ctx'=8] {'ctx'}, use_global_device_ids=true, to_apply=%region_16.17 | all-reduce | flops 2304 | bytes 9216 | tf_op jit(solution)/shard_map/psum | solution.py:298
  609.8 3.9 convolution_add_fusion.3
  616.4 45.1 %all-reduce.20.cloned.1.call-done = (bf16[192,2304]{1,0:T(8,128)(2,1)}, bf16[192,768]{1,0:T(8,128)(2,1)}, bf16[192,3072]{1,0:T(8,128)(2,1)}, bf16[768,768]{1,0:T(8,128)(2,1)}) async-done(((bf16[192,2304]{1,0:T(8,128)(2,1)}, bf16[192,768]{1,0:T(8,128)(2,1)}, bf16[192,3072]{1,0:T(8,128)(2,1)}, bf16[768,768]{1,0:T(8,128)(2,1)}), (bf16[192,2304]{1,0:T(8,128)(2,1)}, bf16[192,768]{1,0:T(8,128)(2,1)}, ...) | async-done | bytes 3538960 | tf_op jit(solution)/shard_map/psum | solution.py:297
  661.5 3.1 convert_element_type.271
  (483 shorter events, 206.7 us)
Async XLA Ops:
  7.2 52.8 %all-gather.8.cloned.1.call-start = ((), (), s32[]{:S(2)}) async-start(), calls=%async_computation.4 | async-start | bytes 4423680 | tf_op jit(solution)/shard_map/all_gather | solution.py:109
  7.9 166.4 %all-gather.10.cloned.1.call-start = ((), (), s32[]{:S(2)}) async-start(), calls=%async_computation.5 | async-start | bytes 3538944 | tf_op jit(solution)/shard_map/all_gather | solution.py:171
  33.2 31.4 %copy-start.32 = (f32[768]{0:T(1024)}, f32[768]{0:T(1024)S(1)}, u32[]{:S(2)}) copy-start(f32[768]{0:T(1024)S(1)} %convert_element_type.241) | copy-start | bytes 9220
  33.2 31.4 %copy-start.38 = (f32[768]{0:T(1024)}, f32[768]{0:T(1024)S(1)}, u32[]{:S(2)}) copy-start(f32[768]{0:T(1024)S(1)} %convert_element_type.242) | copy-start | bytes 9220
  34.7 32.3 %copy-start.36 = (f32[256,16]{0,1:T(8,128)}, f32[256,16]{0,1:T(8,128)S(1)}, u32[]{:S(2)}) copy-start(f32[256,16]{0,1:T(8,128)S(1)} %get-tuple-element.582) | copy-start | bytes 49156
  35.8 28.8 %copy-start.41 = (f32[256]{0:T(256)}, f32[256]{0:T(256)S(1)}, u32[]{:S(2)}) copy-start(f32[256]{0:T(256)S(1)} %broadcast_multiply_fusion.1) | copy-start | bytes 3076
  37.1 27.6 %copy-start.50 = (f32[256]{0:T(256)}, f32[256]{0:T(256)S(1)}, u32[]{:S(2)}) copy-start(f32[256]{0:T(256)S(1)} %fusion.73) | copy-start | bytes 3076
  37.1 27.6 %copy-start.44 = (f32[256]{0:T(256)}, f32[256]{0:T(256)S(1)}, u32[]{:S(2)}) copy-start(f32[256]{0:T(256)S(1)} %fusion.109) | copy-start | bytes 3076
  68.5 172.0 %all-gather.14.cloned.1.call-start = ((), (), s32[]{:S(2)}) async-start(), calls=%async_computation.7 | async-start | bytes 5898240 | tf_op jit(solution)/shard_map/all_gather | solution.py:113
  69.2 182.7 %all-gather.16.cloned.1.call-start = ((), (), s32[]{:S(2)}) async-start(), calls=%async_computation.8 | async-start | bytes 5898240 | tf_op jit(solution)/shard_map/all_gather | solution.py:115
  69.8 194.8 %all-gather.12.cloned.1.call-start = ((), (), s32[]{:S(2)}) async-start(), calls=%async_computation.6 | async-start | bytes 1474560 | tf_op jit(solution)/shard_map/all_gather | solution.py:111
  70.7 9.3 %collective-permute-start.4 = (bf16[256,12,64]{0,2,1:T(8,128)(2,1)}, bf16[256,12,64]{0,2,1:T(8,128)(2,1)S(1)}, u32[]{:S(2)}, u32[]{:S(2)}) collective-permute-start(bf16[256,12,64]{0,2,1:T(8,128)(2,1)} %fusion.81), channel_id=1, source_target_pairs={{0,1},{1,2},{2,3},{3,4},{4,5},{5,6},{6,7},{7,0},{8,9},{9,10},{10,1... | collective-permute-start | bytes 1179656 | tf_op jit(solution)/shard_map/ppermute | solution.py:174
  80.0 17.3 %collective-permute-start.5 = (bf16[256,12,64]{0,2,1:T(8,128)(2,1)S(1)}, bf16[256,12,64]{0,2,1:T(8,128)(2,1)S(1)}, u32[]{:S(2)}, u32[]{:S(2)}) collective-permute-start(bf16[256,12,64]{0,2,1:T(8,128)(2,1)S(1)} %collective-permute-done.4), channel_id=1, source_target_pairs={{0,1},{1,2},{2,3},{3,4},{4,5},{5,6},{6,7},{7,0},{8,9},{9,10},{10,1... | collective-permute-start | bytes 1179656 | tf_op jit(solution)/shard_map/ppermute | solution.py:174
  98.0 16.6 %collective-permute-start.6 = (bf16[256,12,64]{0,2,1:T(8,128)(2,1)S(1)}, bf16[256,12,64]{0,2,1:T(8,128)(2,1)S(1)}, u32[]{:S(2)}, u32[]{:S(2)}) collective-permute-start(bf16[256,12,64]{0,2,1:T(8,128)(2,1)S(1)} %collective-permute-done.5), channel_id=1, source_target_pairs={{0,1},{1,2},{2,3},{3,4},{4,5},{5,6},{6,7},{7,0},{8,9},{9,10},{10,1... | collective-permute-start | bytes 1179656 | tf_op jit(solution)/shard_map/ppermute | solution.py:174
  115.3 9.0 %collective-permute-start.7 = (bf16[256,12,64]{0,2,1:T(8,128)(2,1)S(1)}, bf16[256,12,64]{0,2,1:T(8,128)(2,1)S(1)}, u32[]{:S(2)}, u32[]{:S(2)}) collective-permute-start(bf16[256,12,64]{0,2,1:T(8,128)(2,1)S(1)} %collective-permute-done.6), channel_id=1, source_target_pairs={{0,1},{1,2},{2,3},{3,4},{4,5},{5,6},{6,7},{7,0},{8,9},{9,10},{10,1... | collective-permute-start | bytes 1179656 | tf_op jit(solution)/shard_map/ppermute | solution.py:174
  125.1 9.0 %collective-permute-start.8 = (bf16[256,12,64]{0,2,1:T(8,128)(2,1)S(1)}, bf16[256,12,64]{0,2,1:T(8,128)(2,1)S(1)}, u32[]{:S(2)}, u32[]{:S(2)}) collective-permute-start(bf16[256,12,64]{0,2,1:T(8,128)(2,1)S(1)} %collective-permute-done.7), channel_id=1, source_target_pairs={{0,1},{1,2},{2,3},{3,4},{4,5},{5,6},{6,7},{7,0},{8,9},{9,10},{10,1... | collective-permute-start | bytes 1179656 | tf_op jit(solution)/shard_map/ppermute | solution.py:174
  134.8 9.1 %collective-permute-start.9 = (bf16[256,12,64]{0,2,1:T(8,128)(2,1)S(1)}, bf16[256,12,64]{0,2,1:T(8,128)(2,1)}, u32[]{:S(2)}, u32[]{:S(2)}) collective-permute-start(bf16[256,12,64]{0,2,1:T(8,128)(2,1)S(1)} %collective-permute-done.8), channel_id=1, source_target_pairs={{0,1},{1,2},{2,3},{3,4},{4,5},{5,6},{6,7},{7,0},{8,9},{9,10},{10,1... | collective-permute-start | bytes 1179656 | tf_op jit(solution)/shard_map/ppermute | solution.py:174
  143.9 23.3 %collective-permute-start.10 = (bf16[256,12,64]{0,2,1:T(8,128)(2,1)}, bf16[256,12,64]{0,2,1:T(8,128)(2,1)}, u32[]{:S(2)}, u32[]{:S(2)}) collective-permute-start(bf16[256,12,64]{0,2,1:T(8,128)(2,1)} %collective-permute-done.9), channel_id=1, source_target_pairs={{0,1},{1,2},{2,3},{3,4},{4,5},{5,6},{6,7},{7,0},{8,9},{9,10},{10,1... | collective-permute-start | bytes 1179656 | tf_op jit(solution)/shard_map/ppermute | solution.py:174
  144.0 394.7 %reduce-scatter.7.cloned.1.call-start = ((), (), s32[]{:S(2)}) async-start(), calls=%async_computation.10 | async-start | bytes 1474560 | tf_op jit(solution)/shard_map/reduce_scatter | solution.py:268
  156.1 13.3 %copy-start.18 = (bf16[256,12,64]{0,2,1:T(8,128)(2,1)S(1)}, bf16[256,12,64]{0,2,1:T(8,128)(2,1)}, u32[]{:S(2)}) copy-start(bf16[256,12,64]{0,2,1:T(8,128)(2,1)} %copy-done.17) | copy-start | bytes 1179652
  156.1 13.4 %copy-start.16 = (bf16[256,12,64]{0,2,1:T(8,128)(2,1)S(1)}, bf16[256,12,64]{0,2,1:T(8,128)(2,1)}, u32[]{:S(2)}) copy-start(bf16[256,12,64]{0,2,1:T(8,128)(2,1)} %copy-done.15) | copy-start | bytes 1179652
  174.3 64.4 %copy-start.4 = (bf16[1,256,768]{2,1,0:T(8,128)(2,1)S(1)}, bf16[1,256,768]{2,1,0:T(8,128)(2,1)}, u32[]{:S(2)}) copy-start(bf16[1,256,768]{2,1,0:T(8,128)(2,1)} %param.33) | copy-start | bytes 1179652
  238.5 13.4 %copy-start.26 = (f32[12,256]{1,0:T(8,128)}, f32[12,256]{1,0:T(8,128)S(1)}, u32[]{:S(2)}) copy-start(f32[12,256]{1,0:T(8,128)S(1)} %get-tuple-element.380) | copy-start | bytes 36868
  240.2 298.4 %reduce-scatter.9.cloned.1.call-start = ((), (), s32[]{:S(2)}) async-start(), calls=%async_computation.11 | async-start | bytes 5898240 | tf_op jit(solution)/shard_map/reduce_scatter | solution.py:274
  252.0 17.1 %copy-start.9 = (bf16[256,3072]{1,0:T(8,128)(2,1)}, bf16[256,3072]{1,0:T(8,128)(2,1)S(1)}, u32[]{:S(2)}) copy-start(bf16[256,3072]{1,0:T(8,128)(2,1)S(1)} %get-tuple-element.560) | copy-start | bytes 4718596
  264.5 274.2 %reduce-scatter.11.cloned.1.call-start = ((), (), s32[]{:S(2)}) async-start(), calls=%async_computation.12 | async-start | bytes 5898240 | tf_op jit(solution)/shard_map/reduce_scatter | solution.py:280
  272.6 300.5 %reduce-scatter.5.cloned.1.call-start = ((), (), s32[]{:S(2)}) async-start(), calls=%async_computation.9 | async-start | bytes 4423680 | tf_op jit(solution)/shard_map/reduce_scatter | solution.py:262
  276.0 247.3 %copy-start.37 = (f32[256,16]{0,1:T(8,128)S(1)}, f32[256,16]{0,1:T(8,128)}, u32[]{:S(2)}) copy-start(f32[256,16]{0,1:T(8,128)} %copy-done.36) | copy-start | bytes 49156
  284.7 9.3 %collective-permute-start.2 = (bf16[256,12,64]{0,2,1:T(8,128)(2,1)}, bf16[256,12,64]{0,2,1:T(8,128)(2,1)}, u32[]{:S(2)}, u32[]{:S(2)}) collective-permute-start(bf16[256,12,64]{0,2,1:T(8,128)(2,1)} %fusion.190), channel_id=1, source_target_pairs={{0,1},{1,2},{2,3},{3,4},{4,5},{5,6},{6,7},{7,0},{8,9},{9,10},{10,1... | collective-permute-start | bytes 1179656 | tf_op jit(solution)/shard_map/while/body/eval_jaxpr/ppermute | solution.py:15
  287.5 10.7 %collective-permute-start.3 = (bf16[256,12,64]{0,2,1:T(8,128)(2,1)}, bf16[256,12,64]{0,2,1:T(8,128)(2,1)}, u32[]{:S(2)}, u32[]{:S(2)}) collective-permute-start(bf16[256,12,64]{0,2,1:T(8,128)(2,1)} %fusion.191), channel_id=1, source_target_pairs={{0,1},{1,2},{2,3},{3,4},{4,5},{5,6},{6,7},{7,0},{8,9},{9,10},{10,1... | collective-permute-start | bytes 1179656 | tf_op jit(solution)/shard_map/while/body/eval_jaxpr/ppermute | solution.py:15
  288.7 13.8 %collective-permute-start = (bf16[256,12,64]{0,2,1:T(8,128)(2,1)S(1)}, bf16[256,12,64]{0,2,1:T(8,128)(2,1)}, u32[]{:S(2)}, u32[]{:S(2)}) collective-permute-start(bf16[256,12,64]{0,2,1:T(8,128)(2,1)S(1)} %copy.91), channel_id=1, source_target_pairs={{0,1},{1,2},{2,3},{3,4},{4,5},{5,6},{6,7},{7,0},{8,9},{9,10},{10,1... | collective-permute-start | bytes 1179656 | tf_op jit(solution)/shard_map/while/body/eval_jaxpr/ppermute | solution.py:15
  288.9 17.7 %collective-permute-start.1 = (bf16[256,12,64]{0,2,1:T(8,128)(2,1)}, bf16[256,12,64]{0,2,1:T(8,128)(2,1)}, u32[]{:S(2)}, u32[]{:S(2)}) collective-permute-start(bf16[256,12,64]{0,2,1:T(8,128)(2,1)} %copy.92), channel_id=1, source_target_pairs={{0,1},{1,2},{2,3},{3,4},{4,5},{5,6},{6,7},{7,0},{8,9},{9,10},{10,1... | collective-permute-start | bytes 1179656 | tf_op jit(solution)/shard_map/while/body/eval_jaxpr/ppermute | solution.py:15
  315.4 9.3 %collective-permute-start.2 = (bf16[256,12,64]{0,2,1:T(8,128)(2,1)}, bf16[256,12,64]{0,2,1:T(8,128)(2,1)}, u32[]{:S(2)}, u32[]{:S(2)}) collective-permute-start(bf16[256,12,64]{0,2,1:T(8,128)(2,1)} %fusion.190), channel_id=1, source_target_pairs={{0,1},{1,2},{2,3},{3,4},{4,5},{5,6},{6,7},{7,0},{8,9},{9,10},{10,1... | collective-permute-start | bytes 1179656 | tf_op jit(solution)/shard_map/while/body/eval_jaxpr/ppermute | solution.py:15
  318.1 10.9 %collective-permute-start.3 = (bf16[256,12,64]{0,2,1:T(8,128)(2,1)}, bf16[256,12,64]{0,2,1:T(8,128)(2,1)}, u32[]{:S(2)}, u32[]{:S(2)}) collective-permute-start(bf16[256,12,64]{0,2,1:T(8,128)(2,1)} %fusion.191), channel_id=1, source_target_pairs={{0,1},{1,2},{2,3},{3,4},{4,5},{5,6},{6,7},{7,0},{8,9},{9,10},{10,1... | collective-permute-start | bytes 1179656 | tf_op jit(solution)/shard_map/while/body/eval_jaxpr/ppermute | solution.py:15
  318.1 15.1 %collective-permute-start = (bf16[256,12,64]{0,2,1:T(8,128)(2,1)S(1)}, bf16[256,12,64]{0,2,1:T(8,128)(2,1)}, u32[]{:S(2)}, u32[]{:S(2)}) collective-permute-start(bf16[256,12,64]{0,2,1:T(8,128)(2,1)S(1)} %copy.91), channel_id=1, source_target_pairs={{0,1},{1,2},{2,3},{3,4},{4,5},{5,6},{6,7},{7,0},{8,9},{9,10},{10,1... | collective-permute-start | bytes 1179656 | tf_op jit(solution)/shard_map/while/body/eval_jaxpr/ppermute | solution.py:15
  318.1 19.3 %collective-permute-start.1 = (bf16[256,12,64]{0,2,1:T(8,128)(2,1)}, bf16[256,12,64]{0,2,1:T(8,128)(2,1)}, u32[]{:S(2)}, u32[]{:S(2)}) collective-permute-start(bf16[256,12,64]{0,2,1:T(8,128)(2,1)} %copy.92), channel_id=1, source_target_pairs={{0,1},{1,2},{2,3},{3,4},{4,5},{5,6},{6,7},{7,0},{8,9},{9,10},{10,1... | collective-permute-start | bytes 1179656 | tf_op jit(solution)/shard_map/while/body/eval_jaxpr/ppermute | solution.py:15
  346.0 9.3 %collective-permute-start.2 = (bf16[256,12,64]{0,2,1:T(8,128)(2,1)}, bf16[256,12,64]{0,2,1:T(8,128)(2,1)}, u32[]{:S(2)}, u32[]{:S(2)}) collective-permute-start(bf16[256,12,64]{0,2,1:T(8,128)(2,1)} %fusion.190), channel_id=1, source_target_pairs={{0,1},{1,2},{2,3},{3,4},{4,5},{5,6},{6,7},{7,0},{8,9},{9,10},{10,1... | collective-permute-start | bytes 1179656 | tf_op jit(solution)/shard_map/while/body/eval_jaxpr/ppermute | solution.py:15
  348.7 10.9 %collective-permute-start.3 = (bf16[256,12,64]{0,2,1:T(8,128)(2,1)}, bf16[256,12,64]{0,2,1:T(8,128)(2,1)}, u32[]{:S(2)}, u32[]{:S(2)}) collective-permute-start(bf16[256,12,64]{0,2,1:T(8,128)(2,1)} %fusion.191), channel_id=1, source_target_pairs={{0,1},{1,2},{2,3},{3,4},{4,5},{5,6},{6,7},{7,0},{8,9},{9,10},{10,1... | collective-permute-start | bytes 1179656 | tf_op jit(solution)/shard_map/while/body/eval_jaxpr/ppermute | solution.py:15
  348.7 15.1 %collective-permute-start = (bf16[256,12,64]{0,2,1:T(8,128)(2,1)S(1)}, bf16[256,12,64]{0,2,1:T(8,128)(2,1)}, u32[]{:S(2)}, u32[]{:S(2)}) collective-permute-start(bf16[256,12,64]{0,2,1:T(8,128)(2,1)S(1)} %copy.91), channel_id=1, source_target_pairs={{0,1},{1,2},{2,3},{3,4},{4,5},{5,6},{6,7},{7,0},{8,9},{9,10},{10,1... | collective-permute-start | bytes 1179656 | tf_op jit(solution)/shard_map/while/body/eval_jaxpr/ppermute | solution.py:15
  348.7 19.3 %collective-permute-start.1 = (bf16[256,12,64]{0,2,1:T(8,128)(2,1)}, bf16[256,12,64]{0,2,1:T(8,128)(2,1)}, u32[]{:S(2)}, u32[]{:S(2)}) collective-permute-start(bf16[256,12,64]{0,2,1:T(8,128)(2,1)} %copy.92), channel_id=1, source_target_pairs={{0,1},{1,2},{2,3},{3,4},{4,5},{5,6},{6,7},{7,0},{8,9},{9,10},{10,1... | collective-permute-start | bytes 1179656 | tf_op jit(solution)/shard_map/while/body/eval_jaxpr/ppermute | solution.py:15
  376.6 9.3 %collective-permute-start.2 = (bf16[256,12,64]{0,2,1:T(8,128)(2,1)}, bf16[256,12,64]{0,2,1:T(8,128)(2,1)}, u32[]{:S(2)}, u32[]{:S(2)}) collective-permute-start(bf16[256,12,64]{0,2,1:T(8,128)(2,1)} %fusion.190), channel_id=1, source_target_pairs={{0,1},{1,2},{2,3},{3,4},{4,5},{5,6},{6,7},{7,0},{8,9},{9,10},{10,1... | collective-permute-start | bytes 1179656 | tf_op jit(solution)/shard_map/while/body/eval_jaxpr/ppermute | solution.py:15
  379.3 10.9 %collective-permute-start.3 = (bf16[256,12,64]{0,2,1:T(8,128)(2,1)}, bf16[256,12,64]{0,2,1:T(8,128)(2,1)}, u32[]{:S(2)}, u32[]{:S(2)}) collective-permute-start(bf16[256,12,64]{0,2,1:T(8,128)(2,1)} %fusion.191), channel_id=1, source_target_pairs={{0,1},{1,2},{2,3},{3,4},{4,5},{5,6},{6,7},{7,0},{8,9},{9,10},{10,1... | collective-permute-start | bytes 1179656 | tf_op jit(solution)/shard_map/while/body/eval_jaxpr/ppermute | solution.py:15
  379.3 15.1 %collective-permute-start = (bf16[256,12,64]{0,2,1:T(8,128)(2,1)S(1)}, bf16[256,12,64]{0,2,1:T(8,128)(2,1)}, u32[]{:S(2)}, u32[]{:S(2)}) collective-permute-start(bf16[256,12,64]{0,2,1:T(8,128)(2,1)S(1)} %copy.91), channel_id=1, source_target_pairs={{0,1},{1,2},{2,3},{3,4},{4,5},{5,6},{6,7},{7,0},{8,9},{9,10},{10,1... | collective-permute-start | bytes 1179656 | tf_op jit(solution)/shard_map/while/body/eval_jaxpr/ppermute | solution.py:15
  379.3 19.3 %collective-permute-start.1 = (bf16[256,12,64]{0,2,1:T(8,128)(2,1)}, bf16[256,12,64]{0,2,1:T(8,128)(2,1)}, u32[]{:S(2)}, u32[]{:S(2)}) collective-permute-start(bf16[256,12,64]{0,2,1:T(8,128)(2,1)} %copy.92), channel_id=1, source_target_pairs={{0,1},{1,2},{2,3},{3,4},{4,5},{5,6},{6,7},{7,0},{8,9},{9,10},{10,1... | collective-permute-start | bytes 1179656 | tf_op jit(solution)/shard_map/while/body/eval_jaxpr/ppermute | solution.py:15
  407.3 9.3 %collective-permute-start.2 = (bf16[256,12,64]{0,2,1:T(8,128)(2,1)}, bf16[256,12,64]{0,2,1:T(8,128)(2,1)}, u32[]{:S(2)}, u32[]{:S(2)}) collective-permute-start(bf16[256,12,64]{0,2,1:T(8,128)(2,1)} %fusion.190), channel_id=1, source_target_pairs={{0,1},{1,2},{2,3},{3,4},{4,5},{5,6},{6,7},{7,0},{8,9},{9,10},{10,1... | collective-permute-start | bytes 1179656 | tf_op jit(solution)/shard_map/while/body/eval_jaxpr/ppermute | solution.py:15
  410.0 10.9 %collective-permute-start.3 = (bf16[256,12,64]{0,2,1:T(8,128)(2,1)}, bf16[256,12,64]{0,2,1:T(8,128)(2,1)}, u32[]{:S(2)}, u32[]{:S(2)}) collective-permute-start(bf16[256,12,64]{0,2,1:T(8,128)(2,1)} %fusion.191), channel_id=1, source_target_pairs={{0,1},{1,2},{2,3},{3,4},{4,5},{5,6},{6,7},{7,0},{8,9},{9,10},{10,1... | collective-permute-start | bytes 1179656 | tf_op jit(solution)/shard_map/while/body/eval_jaxpr/ppermute | solution.py:15
  410.0 15.1 %collective-permute-start = (bf16[256,12,64]{0,2,1:T(8,128)(2,1)S(1)}, bf16[256,12,64]{0,2,1:T(8,128)(2,1)}, u32[]{:S(2)}, u32[]{:S(2)}) collective-permute-start(bf16[256,12,64]{0,2,1:T(8,128)(2,1)S(1)} %copy.91), channel_id=1, source_target_pairs={{0,1},{1,2},{2,3},{3,4},{4,5},{5,6},{6,7},{7,0},{8,9},{9,10},{10,1... | collective-permute-start | bytes 1179656 | tf_op jit(solution)/shard_map/while/body/eval_jaxpr/ppermute | solution.py:15
  410.0 19.3 %collective-permute-start.1 = (bf16[256,12,64]{0,2,1:T(8,128)(2,1)}, bf16[256,12,64]{0,2,1:T(8,128)(2,1)}, u32[]{:S(2)}, u32[]{:S(2)}) collective-permute-start(bf16[256,12,64]{0,2,1:T(8,128)(2,1)} %copy.92), channel_id=1, source_target_pairs={{0,1},{1,2},{2,3},{3,4},{4,5},{5,6},{6,7},{7,0},{8,9},{9,10},{10,1... | collective-permute-start | bytes 1179656 | tf_op jit(solution)/shard_map/while/body/eval_jaxpr/ppermute | solution.py:15
  437.9 9.3 %collective-permute-start.2 = (bf16[256,12,64]{0,2,1:T(8,128)(2,1)}, bf16[256,12,64]{0,2,1:T(8,128)(2,1)}, u32[]{:S(2)}, u32[]{:S(2)}) collective-permute-start(bf16[256,12,64]{0,2,1:T(8,128)(2,1)} %fusion.190), channel_id=1, source_target_pairs={{0,1},{1,2},{2,3},{3,4},{4,5},{5,6},{6,7},{7,0},{8,9},{9,10},{10,1... | collective-permute-start | bytes 1179656 | tf_op jit(solution)/shard_map/while/body/eval_jaxpr/ppermute | solution.py:15
  440.6 10.9 %collective-permute-start.3 = (bf16[256,12,64]{0,2,1:T(8,128)(2,1)}, bf16[256,12,64]{0,2,1:T(8,128)(2,1)}, u32[]{:S(2)}, u32[]{:S(2)}) collective-permute-start(bf16[256,12,64]{0,2,1:T(8,128)(2,1)} %fusion.191), channel_id=1, source_target_pairs={{0,1},{1,2},{2,3},{3,4},{4,5},{5,6},{6,7},{7,0},{8,9},{9,10},{10,1... | collective-permute-start | bytes 1179656 | tf_op jit(solution)/shard_map/while/body/eval_jaxpr/ppermute | solution.py:15
  440.6 15.1 %collective-permute-start = (bf16[256,12,64]{0,2,1:T(8,128)(2,1)S(1)}, bf16[256,12,64]{0,2,1:T(8,128)(2,1)}, u32[]{:S(2)}, u32[]{:S(2)}) collective-permute-start(bf16[256,12,64]{0,2,1:T(8,128)(2,1)S(1)} %copy.91), channel_id=1, source_target_pairs={{0,1},{1,2},{2,3},{3,4},{4,5},{5,6},{6,7},{7,0},{8,9},{9,10},{10,1... | collective-permute-start | bytes 1179656 | tf_op jit(solution)/shard_map/while/body/eval_jaxpr/ppermute | solution.py:15
  440.6 19.3 %collective-permute-start.1 = (bf16[256,12,64]{0,2,1:T(8,128)(2,1)}, bf16[256,12,64]{0,2,1:T(8,128)(2,1)}, u32[]{:S(2)}, u32[]{:S(2)}) collective-permute-start(bf16[256,12,64]{0,2,1:T(8,128)(2,1)} %copy.92), channel_id=1, source_target_pairs={{0,1},{1,2},{2,3},{3,4},{4,5},{5,6},{6,7},{7,0},{8,9},{9,10},{10,1... | collective-permute-start | bytes 1179656 | tf_op jit(solution)/shard_map/while/body/eval_jaxpr/ppermute | solution.py:15
  468.6 9.3 %collective-permute-start.2 = (bf16[256,12,64]{0,2,1:T(8,128)(2,1)}, bf16[256,12,64]{0,2,1:T(8,128)(2,1)}, u32[]{:S(2)}, u32[]{:S(2)}) collective-permute-start(bf16[256,12,64]{0,2,1:T(8,128)(2,1)} %fusion.190), channel_id=1, source_target_pairs={{0,1},{1,2},{2,3},{3,4},{4,5},{5,6},{6,7},{7,0},{8,9},{9,10},{10,1... | collective-permute-start | bytes 1179656 | tf_op jit(solution)/shard_map/while/body/eval_jaxpr/ppermute | solution.py:15
  471.2 10.9 %collective-permute-start.3 = (bf16[256,12,64]{0,2,1:T(8,128)(2,1)}, bf16[256,12,64]{0,2,1:T(8,128)(2,1)}, u32[]{:S(2)}, u32[]{:S(2)}) collective-permute-start(bf16[256,12,64]{0,2,1:T(8,128)(2,1)} %fusion.191), channel_id=1, source_target_pairs={{0,1},{1,2},{2,3},{3,4},{4,5},{5,6},{6,7},{7,0},{8,9},{9,10},{10,1... | collective-permute-start | bytes 1179656 | tf_op jit(solution)/shard_map/while/body/eval_jaxpr/ppermute | solution.py:15
  471.2 15.1 %collective-permute-start = (bf16[256,12,64]{0,2,1:T(8,128)(2,1)S(1)}, bf16[256,12,64]{0,2,1:T(8,128)(2,1)}, u32[]{:S(2)}, u32[]{:S(2)}) collective-permute-start(bf16[256,12,64]{0,2,1:T(8,128)(2,1)S(1)} %copy.91), channel_id=1, source_target_pairs={{0,1},{1,2},{2,3},{3,4},{4,5},{5,6},{6,7},{7,0},{8,9},{9,10},{10,1... | collective-permute-start | bytes 1179656 | tf_op jit(solution)/shard_map/while/body/eval_jaxpr/ppermute | solution.py:15
  471.2 19.3 %collective-permute-start.1 = (bf16[256,12,64]{0,2,1:T(8,128)(2,1)}, bf16[256,12,64]{0,2,1:T(8,128)(2,1)}, u32[]{:S(2)}, u32[]{:S(2)}) collective-permute-start(bf16[256,12,64]{0,2,1:T(8,128)(2,1)} %copy.92), channel_id=1, source_target_pairs={{0,1},{1,2},{2,3},{3,4},{4,5},{5,6},{6,7},{7,0},{8,9},{9,10},{10,1... | collective-permute-start | bytes 1179656 | tf_op jit(solution)/shard_map/while/body/eval_jaxpr/ppermute | solution.py:15
  499.2 9.3 %collective-permute-start.2 = (bf16[256,12,64]{0,2,1:T(8,128)(2,1)}, bf16[256,12,64]{0,2,1:T(8,128)(2,1)}, u32[]{:S(2)}, u32[]{:S(2)}) collective-permute-start(bf16[256,12,64]{0,2,1:T(8,128)(2,1)} %fusion.190), channel_id=1, source_target_pairs={{0,1},{1,2},{2,3},{3,4},{4,5},{5,6},{6,7},{7,0},{8,9},{9,10},{10,1... | collective-permute-start | bytes 1179656 | tf_op jit(solution)/shard_map/while/body/eval_jaxpr/ppermute | solution.py:15
  501.8 10.9 %collective-permute-start.3 = (bf16[256,12,64]{0,2,1:T(8,128)(2,1)}, bf16[256,12,64]{0,2,1:T(8,128)(2,1)}, u32[]{:S(2)}, u32[]{:S(2)}) collective-permute-start(bf16[256,12,64]{0,2,1:T(8,128)(2,1)} %fusion.191), channel_id=1, source_target_pairs={{0,1},{1,2},{2,3},{3,4},{4,5},{5,6},{6,7},{7,0},{8,9},{9,10},{10,1... | collective-permute-start | bytes 1179656 | tf_op jit(solution)/shard_map/while/body/eval_jaxpr/ppermute | solution.py:15
  501.8 15.1 %collective-permute-start = (bf16[256,12,64]{0,2,1:T(8,128)(2,1)S(1)}, bf16[256,12,64]{0,2,1:T(8,128)(2,1)}, u32[]{:S(2)}, u32[]{:S(2)}) collective-permute-start(bf16[256,12,64]{0,2,1:T(8,128)(2,1)S(1)} %copy.91), channel_id=1, source_target_pairs={{0,1},{1,2},{2,3},{3,4},{4,5},{5,6},{6,7},{7,0},{8,9},{9,10},{10,1... | collective-permute-start | bytes 1179656 | tf_op jit(solution)/shard_map/while/body/eval_jaxpr/ppermute | solution.py:15
  501.8 19.3 %collective-permute-start.1 = (bf16[256,12,64]{0,2,1:T(8,128)(2,1)}, bf16[256,12,64]{0,2,1:T(8,128)(2,1)}, u32[]{:S(2)}, u32[]{:S(2)}) collective-permute-start(bf16[256,12,64]{0,2,1:T(8,128)(2,1)} %copy.92), channel_id=1, source_target_pairs={{0,1},{1,2},{2,3},{3,4},{4,5},{5,6},{6,7},{7,0},{8,9},{9,10},{10,1... | collective-permute-start | bytes 1179656 | tf_op jit(solution)/shard_map/while/body/eval_jaxpr/ppermute | solution.py:15
  528.1 133.4 %all-reduce.20.cloned.1.call-start = ((), (), s32[]{:S(2)}) async-start(), calls=%async_computation.13 | async-start | bytes 7077888 | tf_op jit(solution)/shard_map/psum | solution.py:297
  538.6 36.5 %copy-start.52 = (bf16[3072]{0:T(1024)(128)(2,1)S(1)}, bf16[3072]{0:T(1024)(128)(2,1)}, u32[]{:S(2)}) copy-start(bf16[3072]{0:T(1024)(128)(2,1)} %get-tuple-element.586) | copy-start | bytes 18436
  538.6 71.1 %copy-start.10 = (bf16[256,3072]{1,0:T(8,128)(2,1)S(1)}, bf16[256,3072]{1,0:T(8,128)(2,1)}, u32[]{:S(2)}) copy-start(bf16[256,3072]{1,0:T(8,128)(2,1)} %copy-done.9) | copy-start | bytes 4718596
  607.5 60.9 %copy-start.53 = (f32[192]{0:T(256)}, f32[192]{0:T(256)S(1)}, u32[]{:S(2)}) copy-start(f32[192]{0:T(256)S(1)} %convert_element_type.269) | copy-start | bytes 2308
  (81 other events, 216.0 us)
Sparse Core Ops, SparseCore 0:
  9.9 50.0 all-gather.7
  68.6 47.2 all-gather.9
  117.8 57.7 all-gather.13
  177.2 57.1 all-gather.15
  236.1 27.7 all-gather.11
  267.2 28.5 reduce-scatter.6
  298.8 57.0 reduce-scatter.8
  358.9 57.0 reduce-scatter.10
  528.3 44.8 reduce-scatter.4
  575.6 85.8 all-reduce.19
